TPU v7x, 256 devices: a whole 4x4x8 slice. The times are simulated.
256 devices in a mesh: grp: 16 (over y_lo, x, core), lon: 16 (over y_hi, z).
Axes of the slice: x: 4, y: 4 (y_hi: 2, y_lo: 2; y = y_hi * 2 + y_lo), z: 8, core: 2. Of those that a mesh axis runs over, the one named last changes fastest.
Arguments:
- ensemble: float32 [256, 16, 128, 128], P('grp', None, 'lon'), may hold values from -6 to 6
- courant_east: float32 [16, 128, 128], P(None, 'lon'), may hold values from -0.9 to 0.9
- northward_courant: float32 [16, 128, 128], P(None, 'lon'), may hold values from -0.9 to 0.9
- measured: float32 [64, 1024], P('lon'), may hold values from -6 to 6
- error_variance: float32 [64, 1024], P('lon'), may hold values from 0.25 to 4
- sensor_cell: int32 [64, 1024], P('lon'), may hold values from 0 to 262143, as said below
- sensor_count: int32 [64], P('lon'), may hold values from 256 to 1024, as said below
- perturbation: float32 [256, 64, 1024], P('grp', 'lon'), may hold values from -6 to 6
Outputs:
- analysis: float32 [256, 16, 128, 128], P('grp', None, 'lon')
Inputs may be any that keep to these rules, and one draw needn't show every extreme that they name: Region r observes sensor_count[r] cells in its first slots; one region has exactly 1024 observations and another exactly 256. `sensor_cell`: every slot of region r, used or not, names a cell of region r.
All inputs are finite; a program needn't handle non-finite values.
Results may differ from a plain program's by a relative error of at most 0.00027.
Values sent between devices are 32-bit elements; how exact they have to be, the bound alone decides.
A program may use at most 192 MiB of HBM per device.

v0:
```python
import math

import jax
import jax.numpy as jnp
from jax import lax
from jax.sharding import PartitionSpec as P

REG_DEV = 4


HIGHEST = lax.Precision.HIGHEST


def extended(cells, sides, width):
    for axis, dim in sides:
        count = lax.axis_size(axis)
        head = lax.slice_in_dim(cells, 0, width, axis=dim)
        tail = lax.slice_in_dim(cells, cells.shape[dim] - width, cells.shape[dim], axis=dim)
        cells = jnp.concatenate(
            [
                lax.ppermute(tail, axis, [(i, (i + 1) % count) for i in range(count)]),
                cells,
                lax.ppermute(head, axis, [((i + 1) % count, i) for i in range(count)]),
            ],
            axis=dim,
        )
    return cells


def boundary_step(state_field, courant):
    padded = jnp.pad(state_field, ((0, 0), (0, 0), (0, 0), (1, 1)))
    northern = padded[..., 2:]
    southern = padded[..., :-2]
    return (
        state_field
        - 0.5 * courant * (northern - southern)
        + 0.5 * courant * courant * (northern - 2.0 * state_field + southern)
    )


def solve_members(factor_lower, right_side):
    return jax.scipy.linalg.cho_solve((factor_lower, True), right_side)


def on_device(
    ensemble,
    courant_east,
    northward_courant,
    measured,
    error_variance,
    sensor_cell,
    sensor_count,
    perturbation,
):
    local_members, levels, columns, row_count = ensemble.shape
    ensemble_members = local_members * lax.axis_size("grp")
    inflation_scale = 1.0 / math.sqrt(ensemble_members - 1)
    band_rows = row_count // REG_DEV
    widened = extended(ensemble, (("lon", 2),), 1)
    eastern = widened[:, :, 2:]
    western = widened[:, :, :-2]
    half_time_step = (
        ensemble
        - 0.5 * courant_east * (eastern - western)
        + 0.5 * courant_east * courant_east * (eastern - 2.0 * ensemble + western)
    )
    prior_state = boundary_step(half_time_step, northward_courant)
    ensemble_count = lax.psum(jnp.sum(prior_state, axis=0), "grp")
    member_deviation = prior_state - ensemble_count / ensemble_members
    cycle_columns = columns * lax.axis_size("lon")
    strip_index = lax.axis_index("lon")
    level_index = sensor_cell // (cycle_columns * row_count)
    column_index = sensor_cell // row_count % cycle_columns - strip_index * columns
    row_index = sensor_cell % row_count
    local_grid_cell = ((level_index * columns + column_index) * row_count + row_index).reshape(-1)
    region_count, slot_count = sensor_cell.shape
    seen_anomaly = jnp.take(
        member_deviation.reshape(local_members, -1), local_grid_cell, axis=1
    ).reshape(local_members, region_count, slot_count)
    observed_prior = jnp.take(
        prior_state.reshape(local_members, -1), local_grid_cell, axis=1
    ).reshape(local_members, region_count, slot_count)
    valid = jnp.where(
        lax.broadcasted_iota(jnp.int32, sensor_cell.shape, 1) < sensor_count[:, None], 1, 0
    ).astype(jnp.int32)
    slot_is_valid = valid > 0
    observed = jnp.where(slot_is_valid[None], seen_anomaly * inflation_scale, 0.0)
    observation_misfit = jnp.where(
        slot_is_valid[None], measured[None] + perturbation - observed_prior, 0.0
    )
    variance = jnp.where(slot_is_valid, error_variance, 1.0)
    gathered = lax.all_gather(observed, "grp", axis=0, tiled=True)
    scaled = gathered / variance[None]
    inner_matrix = jnp.einsum("pro,qro->rpq", scaled, gathered, precision=HIGHEST) + jnp.eye(
        ensemble_members, dtype=jnp.float32
    )
    right_side = jnp.einsum("pro,kro->rpk", scaled, observation_misfit, precision=HIGHEST)
    factor_lower = jnp.linalg.cholesky(inner_matrix)
    weights = jax.vmap(solve_members)(factor_lower, right_side)
    start_sum = jnp.zeros((local_members, levels, columns, REG_DEV, band_rows), jnp.float32)
    member_block = lax.all_gather(member_deviation, "grp", axis=0, tiled=True)
    block_size = member_block.shape[0]
    blocks = member_block.reshape(block_size, levels, columns, REG_DEV, band_rows)
    analysis_update = (
        start_sum + jnp.einsum("rpm,plxrb->mlxrb", weights, blocks, precision=HIGHEST)
    ).reshape(ensemble.shape)
    return prior_state + inflation_scale * analysis_update


def solution(mesh):
    return jax.shard_map(
        on_device,
        mesh=mesh,
        in_specs=(
            P("grp", None, "lon", None),
            P(None, "lon", None),
            P(None, "lon", None),
            P("lon", None),
            P("lon", None),
            P("lon", None),
            P("lon"),
            P("grp", "lon", None),
        ),
        out_specs=P("grp", None, "lon", None),
        check_vma=False,
    )
```

profile of v0, /device:TPU:1, one launch (start us, length us, event | category | flops | bytes accessed | tf_op | source)
XLA Modules:
  0.0 512.4 jit_solution(4221203697218236858)
XLA Ops:
  6.5 1.7 fusion.48
  8.3 9.1 %collective-permute-start = (f32[16,16,1,128]{3,1,2,0:T(8,128)S(1)}, f32[16,16,1,128]{3,1,2,0:T(8,128)S(1)}, u32[]{:S(2)}, u32[]{:S(2)}) collective-permute-start(f32[16,16,1,128]{3,1,2,0:T(8,128)S(1)} %bitcast.82), channel_id=1, source_target_pairs={{1,0},{2,1},{3,2},{4,3},{5,4},{6,5},{7,6},{8,7},{9,8},{10,9},{11,1... | collective-permute-start | bytes 393224 | tf_op jit(solution)/shard_map/ppermute | solution.py:23
  18.3 0.9 broadcast_multiply_fusion.1
  19.9 4.9 collective-permute-done.1
  24.8 2.7 multiply_add_fusion.1
  27.5 1.2 fusion.46
  28.9 105.2 %all-reduce.4.cloned.1.call-done = f32[16,8,128]{2,1,0:T(8,128)} async-done(((f32[16,8,128]{2,1,0:T(8,128)}), f32[16,8,128]{2,1,0:T(8,128)}) %all-reduce.4.cloned.1.call-update) | async-done | bytes 65552 | tf_op jit(solution)/shard_map/psum | solution.py:68
  135.1 4.6 copy.91
  139.7 14.2 %gather_fusion = f32[4096,16]{1,0:T(8,128)S(1)} fusion(f32[16,16384]{0,1:T(8,128)} %bitcast.76, s32[4096]{0:T(1024)S(1)} %fusion.43), kind=kCustom, calls=%fused_computation.clone | custom fusion | bytes 540672 | tf_op jit(solution)/shard_map/jit(_take)/gather | solution.py:77
  157.5 4.6 copy.99
  162.1 17.5 %gather_fusion.1 = f32[4096,16]{1,0:T(8,128)} fusion(f32[16,16384]{0,1:T(8,128)} %bitcast.75, s32[4096]{0:T(1024)S(1)} %fusion.43), kind=kCustom, calls=%fused_computation.1.clone | custom fusion | bytes 540672 | tf_op jit(solution)/shard_map/jit(_take)/gather | solution.py:80
  179.6 3.6 broadcast_select_fusion
  183.3 1.3 copy.101
  184.5 13.9 %all-gather.5.cloned.1.call-done = f32[256,4,1024]{2,0,1:T(8,128)} async-done(((f32[16,4,1024]{2,0,1:T(8,128)}), f32[256,4,1024]{2,0,1:T(8,128)}) %all-gather.5.cloned.1.call-update) | async-done | bytes 4194320 | tf_op jit(solution)/shard_map/all_gather | solution.py:92
  198.4 11.5 %fusion.4 = f32[4,256,256]{2,1,0:T(8,128)S(1)} fusion(f32[256,4,1024]{2,0,1:T(8,128)} %all-gather.5.cloned.1.call-done, f32[4,1024]{1,0:T(4,128)S(1)} %copy-done.4), kind=kOutput, calls=%fused_computation.9 | convolution fusion | flops 3222274048 | bytes 5259264 | tf_op jit(solution)/shard_map/pro,qro->rpq/dot_general | solution.py:94
  210.3 1.1 fusion.11
  211.4 1.0 copy-done.1
  212.4 46.9 %custom-call.20 = f32[4,128,128]{2,1,0:T(8,128)S(1)} custom-call(f32[4,128,128]{2,1,0:T(8,128)S(1)} %cholesky.122), custom_call_target="Cholesky" | custom-call | tf_op jit(solution)/shard_map/jit(cholesky)/cholesky | solution.py:98
  259.5 39.5 %custom-call.21 = f32[4,1,128,128]{2,3,1,0:T(8,128)S(1)} custom-call(f32[4,1,128,128]{3,2,1,0:T(8,128)S(1)} %select_bitcast_fusion), custom_call_target="InvertDiagBlocksLowerTriangular" | custom-call | tf_op jit(solution)/shard_map/jit(cholesky)/cholesky | solution.py:98
  299.0 1.4 constant_dynamic-update-slice_fusion.1
  300.3 1.6 convolution_subtract_fusion
  301.9 46.9 %custom-call.22 = f32[4,128,128]{2,1,0:T(8,128)S(1)} custom-call(f32[4,128,128]{2,1,0:T(8,128)S(1)} %convolution_subtract_fusion), custom_call_target="Cholesky" | custom-call | tf_op jit(solution)/shard_map/jit(cholesky)/cholesky | solution.py:98
  349.4 5.6 %while.1 = (s32[]{:T(128)}, f32[4,256,256]{2,1,0:T(8,128)S(1)}, s32[2,2]{1,0:T(2,128)S(1)}, f32[2,4,128,128]{3,2,0,1:T(8,128)}, s32[]{:T(128)}) while((s32[]{:T(128)}, f32[4,256,256]{2,1,0:T(8,128)S(1)}, s32[2,2]{1,0:T(2,128)S(1)}, f32[2,4,128,128]{3,2,0,1:T(8,128)}, s32[]{:T(128)}) %tuple.28), condition=%wide.while_cond, body=%wide.while_body.sunk | while | flops 2 | bytes 525921 | solution.py:42
  350.1 2.1 bitcast_dynamic-update-slice_fusion.2
  352.9 2.1 bitcast_dynamic-update-slice_fusion.2
  355.0 79.4 %custom-call.23 = f32[4,2,128,128]{2,3,1,0:T(8,128)S(1)} custom-call(f32[4,2,128,128]{3,2,1,0:T(8,128)} %bitcast.83), custom_call_target="InvertDiagBlocksLowerTriangular" | custom-call | tf_op jit(solution)/shard_map/vmap(jit(_cho_solve))/triangular_solve | solution.py:42
  434.5 6.1 %fusion.2 = f32[4,256,16]{1,2,0:T(8,128)S(1)} fusion(f32[256,4,1024]{2,0,1:T(8,128)} %all-gather.5.cloned.1.call-done, f32[4,1024]{1,0:T(4,128)S(1)} %copy-done.4, f32[16,4,1024]{2,0,1:T(8,128)S(1)} %copy-done.2, f32[16,4,1024]{2,1,0:T(4,128)} %param.17, f32[4,1024]{1,0:T(4,128)S(1)} %copy-done.6, pred[4,1024]{1,0:T(4,128)(4,1)S(1)} %select_compare_fusion), kind=kOutput, calls=%fused_computation.7 | convolution fusion | flops 202571776 | bytes 4820992 | tf_op jit(solution)/shard_map/pro,kro->rpk/dot_general | solution.py:97
  443.1 18.0 %copy.90 = f32[256,16,8,128]{0,3,2,1:T(8,128)} copy(f32[256,16,8,128]{3,2,1,0:T(8,128)} %all-gather.3.cloned.1.call-done) | data formatting | bytes 33554432 | tf_op jit(solution)/shard_map/all_gather | solution.py:101
  461.1 35.1 %multiply_bitcast_fusion = f32[16,16,8,4,32]{4,0,2,1,3:T(8,128)S(1)} fusion(f32[256,16,8,4,32]{0,4,3,2,1:T(8,128)} %bitcast.74, f32[4,128,16]{1,2,0:T(8,128)S(1)} %fusion.22, f32[4,128,16]{1,2,0:T(8,128)S(1)} %fusion.20), kind=kOutput, calls=%fused_computation.6 | convolution fusion | flops 805584896 | bytes 17891328 | tf_op jit(solution)/shard_map/rpm,plxrb->mlxrb/dot_general | solution.py:105
  496.2 4.7 copy.107
  500.9 3.7 mul.110
  504.6 1.1 add.105
  (59 shorter events, 11.3 us)
Async XLA Ops:
  6.5 22.3 %copy-start.5 = (s32[4]{0:T(128)S(1)}, s32[4]{0:T(128)}, u32[]{:S(2)}) copy-start(s32[4]{0:T(128)} %param.16) | copy-start | bytes 52
  6.5 127.6 %all-reduce.4.cloned.1.call-start = ((), (), s32[]{:S(2)}) async-start(), calls=%async_computation | async-start | bytes 131072 | tf_op jit(solution)/shard_map/psum | solution.py:68
  8.3 11.6 %collective-permute-start = (f32[16,16,1,128]{3,1,2,0:T(8,128)S(1)}, f32[16,16,1,128]{3,1,2,0:T(8,128)S(1)}, u32[]{:S(2)}, u32[]{:S(2)}) collective-permute-start(f32[16,16,1,128]{3,1,2,0:T(8,128)S(1)} %bitcast.82), channel_id=1, source_target_pairs={{1,0},{2,1},{3,2},{4,3},{5,4},{6,5},{7,6},{8,7},{9,8},{10,9},{11,1... | collective-permute-start | bytes 393224 | tf_op jit(solution)/shard_map/ppermute | solution.py:23
  17.4 7.4 %collective-permute-start.1 = (f32[16,16,1,128]{3,1,2,0:T(8,128)S(1)}, f32[16,16,1,128]{3,1,2,0:T(8,128)S(1)}, u32[]{:S(2)}, u32[]{:S(2)}) collective-permute-start(f32[16,16,1,128]{3,1,2,0:T(8,128)S(1)} %bitcast.81), channel_id=1, source_target_pairs={{0,1},{1,2},{2,3},{3,4},{4,5},{5,6},{6,7},{7,8},{8,9},{9,10},{10,1... | collective-permute-start | bytes 393224 | tf_op jit(solution)/shard_map/ppermute | solution.py:21
  28.8 169.7 %all-gather.5.cloned.1.call-start = ((), (), s32[]{:S(2)}) async-start(), calls=%async_computation.2 | async-start | bytes 4456448 | tf_op jit(solution)/shard_map/all_gather | solution.py:92
  135.0 4.7 copy-start
  139.7 17.1 %copy-start.3 = (f32[4,1024]{1,0:T(4,128)S(1)}, f32[4,1024]{1,0:T(4,128)}, u32[]{:S(2)}) copy-start(f32[4,1024]{1,0:T(4,128)} %param.14) | copy-start | bytes 49156
  155.3 287.9 %all-gather.3.cloned.1.call-start = ((), (), s32[]{:S(2)}) async-start(), calls=%async_computation.1 | async-start | bytes 17825792 | tf_op jit(solution)/shard_map/all_gather | solution.py:101
  162.1 36.3 %copy-start.4 = (f32[4,1024]{1,0:T(4,128)S(1)}, f32[4,1024]{1,0:T(4,128)}, u32[]{:S(2)}) copy-start(f32[4,1024]{1,0:T(4,128)} %broadcast_select_fusion.1) | copy-start | bytes 49156
  211.4 1.0 copy-start.1
  259.4 175.1 %copy-start.2 = (f32[16,4,1024]{2,0,1:T(8,128)S(1)}, f32[16,4,1024]{2,0,1:T(8,128)}, u32[]{:S(2)}) copy-start(f32[16,4,1024]{2,0,1:T(8,128)} %copy.101) | copy-start | bytes 786436
  259.4 175.0 %copy-start.6 = (f32[4,1024]{1,0:T(4,128)S(1)}, f32[4,1024]{1,0:T(4,128)}, u32[]{:S(2)}) copy-start(f32[4,1024]{1,0:T(4,128)} %param.13) | copy-start | bytes 49156
Sparse Core Ops, SparseCore 0:
  28.9 105.1 all-reduce.3
  155.4 43.0 all-gather.4
  200.5 94.4 all-gather.2
where the time goes:
time: 517 us; the launch traced here: 512 us
  other arithmetic  229 us (44%)
  waiting for transfers between devices  124 us (24%)
  local copies, waits for them, and re-layouts  78 us (15%)
  matrix products  58.2 us (11%)
  between operations  13.6 us (3%)
  starting transfers between devices  9.67 us (2%)
    another operation x10, other arithmetic, on_device(): factor_lower = jnp.linalg.cholesky(inner_matrix)  134 us
    psum x1, waiting for transfers between devices, on_device(): ensemble_count = lax.psum(jnp.sum(prior_state, axis=0), 'grp')  105 us
    another operation x4, other arithmetic, solve_members(): return jax.scipy.linalg.cho_solve((factor_lower, True), right_side)  79.6 us
    dot_general x1, matrix products, on_device(): jnp.einsum('rpm,plxrb->mlxrb', weights, blocks, precision=HIGHEST)  35.1 us
    all_gather x1, local copies, waits for them, and re-layouts, on_device(): member_block = lax.all_gather(member_deviation, 'grp', axis=0, tiled=True)  18 us
    gather x1, local copies, waits for them, and re-layouts, on_device(): jnp.take(prior_state.reshape(local_members, -1), local_grid_cell, axis=1)  17.5 us
    gather x2, local copies, waits for them, and re-layouts, on_device(): jnp.take(member_deviation.reshape(local_members, -1), local_grid_cell, ax...  14.7 us
    all_gather x1, waiting for transfers between devices, on_device(): gathered = lax.all_gather(observed, 'grp', axis=0, tiled=True)  13.9 us
  transfers between devices with their start and end apart: 5, of which 3 were waited for; matrix products, arithmetic and copies ran while one was open for 54% of the time, Pallas kernels for 0%

commit v1 on v0

v1 whole, which is shorter than its diff:
```python
import functools
import math

import jax
import jax.numpy as jnp
from jax import lax
from jax.experimental import pallas as pl
from jax.experimental.pallas import tpu as pltpu
from jax.sharding import PartitionSpec as P

MESH = pl.DeviceIdType.MESH
F32 = jnp.float32
BF16 = jnp.bfloat16
NG = 16
NS = 16
MB = 16
M = 256
LEV = 16
LON = 8
LAT = 128
NB = 4
NQ = 4
NO = 1024
SCALE = 1.0 / math.sqrt(M - 1)
VMEM = pl.BlockSpec(memory_space=pltpu.VMEM)
SMEM = pl.BlockSpec(memory_space=pltpu.SMEM)


def split2(x):
    hi = x.astype(BF16)
    lo = (x - hi.astype(F32)).astype(BF16)
    return hi, lo


def send_kernel(
    ens_ref, ce_ref, cn_ref, pert_ref, cell_ref,
    zr_ref, pt_ref, ft_ref,
    hsrc, hdst, coef, fp, lhs, zb, pb,
    h_send, h_recv, p_send, p_recv, z_send, z_recv, f_send, f_recv,
):
    g = lax.axis_index("grp")
    s = lax.axis_index("lon")
    my_b, my_q = g // NQ, lax.rem(g, NQ)
    east, west = lax.rem(s + 1, NS), lax.rem(s + NS - 1, NS)

    barrier = pltpu.get_barrier_semaphore()
    for i in range(1, NG):
        pl.semaphore_signal(barrier, inc=1, device_id={"grp": lax.rem(g + i, NG)}, device_id_type=MESH)
    for n in (east, west):
        pl.semaphore_signal(barrier, inc=1, device_id={"lon": n}, device_id_type=MESH)

    hsrc[0] = ens_ref[:, :, LON - 1, :]
    hsrc[1] = ens_ref[:, :, 0, :]
    for b in range(NB):
        pb[b] = pert_ref[:, b, :]
    pl.semaphore_wait(barrier, NG - 1 + 2)

    def halo(i, to):
        return pltpu.make_async_remote_copy(
            src_ref=hsrc.at[i], dst_ref=hdst.at[i], send_sem=h_send.at[i], recv_sem=h_recv.at[i],
            device_id={"lon": to}, device_id_type=MESH)

    halo(0, east).start()
    halo(1, west).start()

    def pert_copy(to):
        return pltpu.make_async_remote_copy(
            src_ref=pb.at[to // NQ], dst_ref=pt_ref.at[pl.ds(g * MB, MB)],
            send_sem=p_send.at[to], recv_sem=p_recv.at[g],
            device_id={"grp": to}, device_id_type=MESH)

    def z_copy(to):
        return pltpu.make_async_remote_copy(
            src_ref=zb.at[to // NQ], dst_ref=zr_ref.at[pl.ds(g * MB, MB)],
            send_sem=z_send.at[to], recv_sem=z_recv.at[g],
            device_id={"grp": to}, device_id_type=MESH)

    def f_copy(to):
        return pltpu.make_async_remote_copy(
            src_ref=fp.at[to], dst_ref=ft_ref.at[:, pl.ds(g * MB, MB), :],
            send_sem=f_send.at[to], recv_sem=f_recv.at[g],
            device_id={"grp": to}, device_id_type=MESH)

    @pl.loop(1, NG)
    def _(i):
        pert_copy(lax.rem(g + i, NG)).start()

    pt_ref[pl.ds(g * MB, MB), :] = pb[my_b]

    lane = lax.broadcasted_iota(jnp.int32, (LON, LAT), 1)
    sub = lax.broadcasted_iota(jnp.int32, (LON, LAT), 0)
    for l in range(LEV):
        c = ce_ref[l]
        coef[0, l] = 1.0 - c * c
        coef[1, l] = 0.5 * (c * c - c)
        coef[2, l] = 0.5 * (c * c + c)
        c = cn_ref[l]
        coef[3, l] = 1.0 - c * c
        coef[4, l] = jnp.where(lane == LAT - 1, 0.0, 0.5 * (c * c - c))
        coef[5, l] = jnp.where(lane == 0, 0.0, 0.5 * (c * c + c))

    halo(0, east).wait()
    halo(1, west).wait()

    block = lane // 32
    for q in range(NQ):
        @pl.loop(0, MB)
        def _(m):
            tiles = []
            for k in range(4):
                l = 4 * q + k
                e = ens_ref[m, l]
                w_edge = jnp.broadcast_to(hdst[0, m, pl.ds(l, 1), :], (LON, LAT))
                e_edge = jnp.broadcast_to(hdst[1, m, pl.ds(l, 1), :], (LON, LAT))
                ww = jnp.where(sub == 0, w_edge, pltpu.roll(e, 1, 0))
                ee = jnp.where(sub == LON - 1, e_edge, pltpu.roll(e, LON - 1, 0))
                half = coef[0, l] * e + coef[1, l] * ee + coef[2, l] * ww
                tiles.append(coef[3, l] * half + coef[4, l] * pltpu.roll(half, LAT - 1, 1)
                             + coef[5, l] * pltpu.roll(half, 1, 1))
            for b in range(NB):
                out = None
                for k in range(4):
                    shift = (32 * (k - b)) % LAT
                    t = pltpu.roll(tiles[k], shift, 1) if shift else tiles[k]
                    out = t if out is None else jnp.where(block == k, t, out)
                for x in range(LON):
                    fp[b * NQ + q, x, pl.ds(m, 1), :] = out[x:x + 1]

    @pl.loop(1, NG)
    def _(i):
        f_copy(lax.rem(g + i, NG)).start()

    ft_ref[:, pl.ds(g * MB, MB), :] = fp[g]

    rows = lax.broadcasted_iota(jnp.int32, (LAT, NO), 0)

    @pl.loop(0, NB)
    def _(i):
        b = lax.rem(my_b + i, NB)
        cell = cell_ref[pl.ds(b, 1), :]
        level = cell // (NS * LON * LAT)
        low = (level % 4) * 32 + cell % 32
        high = (level // 4) * LON + (cell // LAT) % LON
        pick = jnp.where(rows == low, 1.0, 0.0).astype(BF16)
        for o in range(0, NO, 256):
            acc = jnp.zeros((MB, 256), F32)
            hi_o = jnp.broadcast_to(high[:, o:o + 256], (MB, 256))
            pk = pick[:, o:o + 256]
            for q in range(NQ):
                f = fp[b * NQ + q].reshape(LON * MB, LAT)
                h0 = f.astype(BF16)
                r = f - h0.astype(F32)
                h1 = r.astype(BF16)
                h2 = (r - h1.astype(F32)).astype(BF16)
                t = jnp.dot(jnp.concatenate([h0, h1, h2], axis=1),
                            jnp.concatenate([pk, pk, pk], axis=0), preferred_element_type=F32)
                for x in range(LON):
                    acc = acc + jnp.where(hi_o == q * LON + x, t[x * MB:(x + 1) * MB], 0.0)
            zb[b, :, o:o + 256] = acc

        @pl.loop(0, NQ)
        def _(j):
            to = b * NQ + lax.rem(my_q + j, NQ)

            @pl.when(to != g)
            def _():
                z_copy(to).start()

    zr_ref[pl.ds(g * MB, MB), :] = zb[my_b]

    @pl.loop(1, NG)
    def _(i):
        to = lax.rem(g + i, NG)
        src = lax.rem(g + NG - i, NG)
        for make, ref, sem in ((pert_copy, pt_ref, p_recv), (z_copy, zr_ref, z_recv)):
            make(to).wait_send()
            pltpu.make_async_remote_copy(
                src_ref=pb.at[0], dst_ref=ref.at[pl.ds(src * MB, MB)],
                send_sem=p_send.at[to], recv_sem=sem.at[src],
                device_id={"grp": to}, device_id_type=MESH).wait_recv()
        f_copy(to).wait_send()
        pltpu.make_async_remote_copy(
            src_ref=fp.at[0], dst_ref=ft_ref.at[:, pl.ds(src * MB, MB), :],
            send_sem=f_send.at[to], recv_sem=f_recv.at[src],
            device_id={"grp": to}, device_id_type=MESH).wait_recv()


def dot(a, b, dims=((1,), (0,))):
    return lax.dot_general(a, b, (dims, ((), ())), precision=lax.Precision.HIGHEST, preferred_element_type=F32)


def solve_kernel(zr_ref, pt_ref, ft_ref, meas_ref, var_ref, count_ref, an_ref, mat, inv, yt):
    b = lax.axis_index("grp") // NQ
    zr = zr_ref[...]
    mean = jnp.sum(zr, axis=0, keepdims=True) * (1.0 / M)
    slot = lax.broadcasted_iota(jnp.int32, (1, NO), 1)
    weight = jnp.where(slot < count_ref[b], 1.0 / var_ref[pl.ds(b, 1), :], 0.0)
    z = (zr - mean) * SCALE
    zw = z * weight
    d = (meas_ref[pl.ds(b, 1), :] + pt_ref[...]) - zr
    eye = jnp.where(lax.broadcasted_iota(jnp.int32, (M, M), 0) == lax.broadcasted_iota(jnp.int32, (M, M), 1), 1.0, 0.0)
    spread = dot(zw, z, ((1,), (1,)))
    rhs_t = dot(d, zw, ((1,), (1,)))
    bound = jnp.sqrt(jnp.sum(spread * spread)) * 1.0001 + 1.0
    mat[...] = spread + eye

    low = 1.0 / bound
    k = 4.0 / ((1.0 + low) * (1.0 + low))
    inv[...] = (k * low) * ((1.0 + low) * eye - low * mat[...])

    def go_on(low):
        return low < 0.97

    def step(low):
        k = 4.0 / ((1.0 + low) * (1.0 + low))
        x = inv[...]
        r = (1.0 + low) * eye - dot(mat[...], x)
        inv[...] = k * dot(x, r)
        return k * low

    low = lax.while_loop(go_on, step, k * low)
    x = inv[...] * (2.0 / (1.0 + low))
    y = dot(rhs_t, x)
    for _ in range(2):
        y = y + dot(rhs_t - dot(y, mat[...]), x)
    y = y * SCALE
    y0, y1 = split2(y)
    lhs = jnp.concatenate([y0, y0, y1], axis=1)
    for x in range(0, LON, 2):
        f = jnp.concatenate([ft_ref[x], ft_ref[x + 1]], axis=1)
        a = f - jnp.sum(f, axis=0, keepdims=True) * (1.0 / M)
        a0, a1 = split2(a)
        u = f + jnp.dot(lhs, jnp.concatenate([a0, a1, a0], axis=0), preferred_element_type=F32)
        an_ref[x] = u[:, :LAT]
        an_ref[x + 1] = u[:, LAT:]


def return_kernel(an_ref, out_ref, rb, send, recv):
    g = lax.axis_index("grp")
    barrier = pltpu.get_barrier_semaphore()
    for i in range(1, NG):
        pl.semaphore_signal(barrier, inc=1, device_id={"grp": lax.rem(g + i, NG)}, device_id_type=MESH)
    pl.semaphore_wait(barrier, NG - 1)

    def copy(to):
        return pltpu.make_async_remote_copy(
            src_ref=an_ref.at[:, pl.ds(to * MB, MB), :], dst_ref=rb.at[g],
            send_sem=send.at[to], recv_sem=recv.at[g],
            device_id={"grp": to}, device_id_type=MESH)

    @pl.loop(1, NG)
    def _(i):
        copy(lax.rem(g + i, NG)).start()

    rb[g] = an_ref[:, pl.ds(g * MB, MB), :]

    @pl.loop(1, NG)
    def _(i):
        to = lax.rem(g + i, NG)
        src = lax.rem(g + NG - i, NG)
        copy(to).wait_send()
        pltpu.make_async_remote_copy(
            src_ref=rb.at[g], dst_ref=rb.at[src], send_sem=send.at[to], recv_sem=recv.at[src],
            device_id={"grp": to}, device_id_type=MESH).wait_recv()

    block = lax.broadcasted_iota(jnp.int32, (LON, LAT), 1) // 32
    for q in range(NQ):
        @pl.loop(0, MB)
        def _(m):
            tiles = []
            for b in range(NB):
                tiles.append(jnp.concatenate([rb[b * NQ + q, x, pl.ds(m, 1), :] for x in range(LON)], axis=0))
            for k in range(4):
                out = None
                for b in range(NB):
                    shift = (32 * (b - k)) % LAT
                    t = pltpu.roll(tiles[b], shift, 1) if shift else tiles[b]
                    out = t if out is None else jnp.where(block == b, t, out)
                out_ref[m, 4 * q + k] = out


def on_device(ensemble, courant_east, northward_courant, measured, error_variance, sensor_cell, sensor_count, perturbation):
    dma = pltpu.SemaphoreType.DMA
    zr, pt, ft = pl.pallas_call(
        send_kernel,
        out_shape=(
            jax.ShapeDtypeStruct((M, NO), F32),
            jax.ShapeDtypeStruct((M, NO), F32),
            jax.ShapeDtypeStruct((LON, M, LAT), F32),
        ),
        in_specs=[VMEM] * 5,
        out_specs=(VMEM,) * 3,
        scratch_shapes=[
            pltpu.VMEM((2, MB, LEV, LAT), F32),
            pltpu.VMEM((2, MB, LEV, LAT), F32),
            pltpu.VMEM((6, LEV, LON, LAT), F32),
            pltpu.VMEM((NG, LON, MB, LAT), F32),
            pltpu.VMEM((LON * MB, 3 * LAT), BF16),
            pltpu.VMEM((NB, MB, NO), F32),
            pltpu.VMEM((NB, MB, NO), F32),
            dma((2,)), dma((2,)), dma((NG,)), dma((NG,)), dma((NG,)), dma((NG,)), dma((NG,)), dma((NG,)),
        ],
        compiler_params=pltpu.CompilerParams(collective_id=0, has_side_effects=True, vmem_limit_bytes=48 << 20),
    )(ensemble, courant_east, northward_courant, perturbation, sensor_cell)
    an = pl.pallas_call(
        solve_kernel,
        out_shape=jax.ShapeDtypeStruct((LON, M, LAT), F32),
        in_specs=[VMEM] * 5 + [SMEM],
        out_specs=VMEM,
        scratch_shapes=[pltpu.VMEM((M, M), F32), pltpu.VMEM((M, M), F32), pltpu.VMEM((M, M), F32)],
        compiler_params=pltpu.CompilerParams(vmem_limit_bytes=48 << 20),
    )(zr, pt, ft, measured, error_variance, sensor_count)
    return pl.pallas_call(
        return_kernel,
        out_shape=jax.ShapeDtypeStruct((MB, LEV, LON, LAT), F32),
        in_specs=[VMEM],
        out_specs=VMEM,
        scratch_shapes=[pltpu.VMEM((NG, LON, MB, LAT), F32), dma((NG,)), dma((NG,))],
        compiler_params=pltpu.CompilerParams(collective_id=1, has_side_effects=True, vmem_limit_bytes=48 << 20),
    )(an)


def solution(mesh):
    return jax.shard_map(
        on_device,
        mesh=mesh,
        in_specs=(
            P("grp", None, "lon", None),
            P(None, "lon", None),
            P(None, "lon", None),
            P("lon", None),
            P("lon", None),
            P("lon", None),
            P("lon"),
            P("grp", "lon", None),
        ),
        out_specs=P("grp", None, "lon", None),
        check_vma=False,
    )
```

time: 517 us -> 97.2 us (0.19)
  other arithmetic: 229 us -> 0 us
  waiting for transfers between devices: 124 us -> 0 us
  Pallas kernels: 0 us -> 90.7 us
  local copies, waits for them, and re-layouts: 78 us -> 6.18 us
  matrix products: 58.2 us -> 0 us
  between operations: 13.6 us -> 0.06 us
  starting transfers between devices: 9.67 us -> 0 us
    another operation x14 -> x0, other arithmetic: 213 us -> none  [the longest x10 134 us: on_device(): factor_lower = jnp.linalg.cholesky(inner_matrix)]
    psum x1 -> x0, waiting for transfers between devices: 105 us -> none  [on_device(): ensemble_count = lax.psum(jnp.sum(prior_state, axis=0), 'grp')]
    pallas_call x0 -> x3, Pallas kernels: none -> 90.7 us  [the longest x1 53.9 us: on_device(): pl.pallas_call(send_kernel, out_shape=(jax.ShapeDtypeStruct((M, NO), F32)...]
    dot_general x3 -> x0, matrix products: 52.7 us -> none  [the longest x1 35.1 us: on_device(): jnp.einsum('rpm,plxrb->mlxrb', weights, blocks, precision=HIGHEST)]
    gather x3 -> x0, local copies, waits for them, and re-layouts: 32.2 us -> none  [the longest x1 17.5 us: on_device(): jnp.take(prior_state.reshape(local_members, -1), local_grid_cell, axis=1)]
    all_gather x1 -> x0, local copies, waits for them, and re-layouts: 18 us -> none  [on_device(): member_block = lax.all_gather(member_deviation, 'grp', axis=0, tiled=True)]
    all_gather x2 -> x0, waiting for transfers between devices: 13.9 us -> none  [the longest x1 13.9 us: on_device(): gathered = lax.all_gather(observed, 'grp', axis=0, tiled=True)]
    ppermute x2 -> x0, starting transfers between devices: 9.12 us -> none  [the longest x1 9.11 us: extended(): lax.ppermute(head, axis, [((i + 1) % count, i) for i in range(count)])]
  transfers between devices with their start and end apart: 5 -> 0, of which waited for: 3 -> 0; matrix products, arithmetic and copies ran while one was open for 54% -> 0% of each run, Pallas kernels for 0% -> 0%
where the time goes in v1:
time: 97.2 us; the launch traced here: 96.9 us
  Pallas kernels  90.7 us (93%)
  local copies, waits for them, and re-layouts  6.18 us (6%)
    pallas_call x1, Pallas kernels, on_device(): pl.pallas_call(send_kernel, out_shape=(jax.ShapeDtypeStruct((M, NO), F32)...  53.9 us
    pallas_call x1, Pallas kernels, on_device(): pl.pallas_call(return_kernel, out_shape=jax.ShapeDtypeStruct((MB, LEV, LO...  26.4 us
    pallas_call x1, Pallas kernels, on_device(): pl.pallas_call(solve_kernel, out_shape=jax.ShapeDtypeStruct((LON, M, LAT)...  10.4 us
    unnamed x17, local copies, waits for them, and re-layouts  6.18 us

profile of v1, /device:TPU:1, one launch (start us, length us, event | category | flops | bytes accessed | tf_op | source)
XLA Modules:
  0.0 96.9 jit_solution(224454675071310538)
XLA Ops:
  0.0 0.0 copy-start
  0.0 1.2 %copy-done = f32[16,16,8,128]{3,2,1,0:T(8,128)S(1)} copy-done((f32[16,16,8,128]{3,2,1,0:T(8,128)S(1)}, f32[16,16,8,128]{3,2,1,0:T(8,128)}, u32[]{:S(2)}) %copy-start) | copy-done | bytes 1048600
  1.2 0.0 copy-start.1
  1.2 0.9 copy-done.1
  2.2 0.0 copy-start.2
  2.2 0.8 copy-done.2
  3.0 0.0 copy-start.3
  3.0 0.8 copy-done.3
  3.9 0.0 copy-start.4
  3.9 0.7 copy-done.4
  4.6 0.0 copy-start.5
  4.6 0.0 copy-start.6
  4.6 53.9 %shard_map.82 = (f32[256,1024]{1,0:T(8,128)S(1)}, f32[256,1024]{1,0:T(8,128)S(1)}, f32[8,256,128]{2,1,0:T(8,128)S(1)}) custom-call(f32[16,16,8,128]{3,2,1,0:T(8,128)S(1)} %copy-done, f32[16,8,128]{2,1,0:T(8,128)S(1)} %copy-done.2, f32[16,8,128]{2,1,0:T(8,128)S(1)} %copy-done.3, f32[16,4,1024]{2,1,0:T(4,128)S(1)} %copy-done.1, s32[4,1024]{1,0:T(4,128)S(1)} %copy-done.4), custom_call_target="tpu_custom_call" | custom-call | tf_op jit(solution)/shard_map/pallas_call | solution.py:284
  58.5 0.0 copy-start.7
  58.5 0.0 copy-done.5
  58.5 0.0 copy-done.6
  58.5 0.6 copy-done.7
  59.1 10.4 %shard_map.83.an_ref = f32[8,256,128]{2,1,0:T(8,128)S(1)} custom-call(f32[256,1024]{1,0:T(8,128)S(1)} %get-tuple-element.8.zr_ref, f32[256,1024]{1,0:T(8,128)S(1)} %get-tuple-element.9.pt_ref, f32[8,256,128]{2,1,0:T(8,128)S(1)} %get-tuple-element.10.ft_ref, f32[4,1024]{1,0:T(4,128)S(1)} %copy-done.5, f32[4,1024]{1,0:T(4,128)S(1)} %copy-done.6, s32[4]{0:T(128)S(1)} %copy-done.7), custom_call_target="tpu_custom_call" | custom-call | tf_op jit(solution)/shard_map/pallas_call | solution.py:305
  69.6 26.4 %shard_map.84 = f32[16,16,8,128]{3,2,1,0:T(8,128)S(1)} custom-call(f32[8,256,128]{2,1,0:T(8,128)S(1)} %shard_map.83.an_ref), custom_call_target="tpu_custom_call" | custom-call | tf_op jit(solution)/shard_map/pallas_call | solution.py:313
  96.0 1.0 %copy.10 = f32[16,16,8,128]{3,2,1,0:T(8,128)} copy(f32[16,16,8,128]{3,2,1,0:T(8,128)S(1)} %shard_map.84) | data formatting | bytes 2097152
Async XLA Ops:
  0.0 1.2 %copy-start = (f32[16,16,8,128]{3,2,1,0:T(8,128)S(1)}, f32[16,16,8,128]{3,2,1,0:T(8,128)}, u32[]{:S(2)}) copy-start(f32[16,16,8,128]{3,2,1,0:T(8,128)} %ens_ref.1) | copy-start | bytes 3145732
  1.2 0.9 copy-start.1
  2.2 0.8 copy-start.2
  3.0 0.8 copy-start.3
  3.9 0.7 copy-start.4
  4.6 53.9 %copy-start.5 = (f32[4,1024]{1,0:T(4,128)S(1)}, f32[4,1024]{1,0:T(4,128)}, u32[]{:S(2)}) copy-start(f32[4,1024]{1,0:T(4,128)} %meas_ref.1) | copy-start | bytes 49156
  4.6 53.9 %copy-start.6 = (f32[4,1024]{1,0:T(4,128)S(1)}, f32[4,1024]{1,0:T(4,128)}, u32[]{:S(2)}) copy-start(f32[4,1024]{1,0:T(4,128)} %var_ref.1) | copy-start | bytes 49156
  58.5 0.7 copy-start.7

commit v2 on v0

v2 whole, which is shorter than its diff:
```python
import functools
import math

import jax
import jax.numpy as jnp
from jax import lax
from jax.experimental import pallas as pl
from jax.experimental.pallas import tpu as pltpu
from jax.sharding import PartitionSpec as P

MESH = pl.DeviceIdType.MESH
F32 = jnp.float32
BF16 = jnp.bfloat16
NG = 16
NS = 16
MB = 16
M = 256
LEV = 16
LON = 8
LAT = 128
NB = 4
NQ = 4
NO = 1024
HO = NO // 2
HX = LON // 2
SCALE = 1.0 / math.sqrt(M - 1)
UNROLL = 4


def split2(x):
    hi = x.astype(BF16)
    lo = (x - hi.astype(F32)).astype(BF16)
    return hi, lo


def dot6(a, b, dims=((1,), (0,))):
    return lax.dot_general(a, b, (dims, ((), ())), precision=lax.Precision.HIGHEST, preferred_element_type=F32)


def dot3(a, b):
    a0, a1 = split2(a)
    b0, b1 = split2(b)
    return jnp.dot(jnp.concatenate([a0, a0, a1], axis=1), jnp.concatenate([b0, b1, b0], axis=0),
                   preferred_element_type=F32)


def swap_blocks(t, upper, odd):
    u = [None] * 4
    for i in (0, 1):
        u[i] = jnp.where(upper, pltpu.roll(t[i + 2], 64, 1), t[i])
        u[i + 2] = jnp.where(upper, t[i + 2], pltpu.roll(t[i], 64, 1))
    v = [None] * 4
    for i in (0, 2):
        v[i] = jnp.where(odd, pltpu.roll(u[i + 1], 32, 1), u[i])
        v[i + 1] = jnp.where(odd, u[i + 1], pltpu.roll(u[i], 96, 1))
    return v


def kernel(
    ens_hbm, ce_hbm, cn_hbm, pert_hbm, cell_hbm, meas_hbm, var_hbm, count_ref,
    out_ref,
    ens, ce, cn, pert, cell_ref, meas, var, hsrc, hdst, coef, fp, zb, pb, zr, pt, ft, an, rb, mat, rhs, inv,
    load, h_send, h_recv, p_send, p_recv, pf_send, pf_recv, z_send, z_recv, zf_send, zf_recv,
    f_send, f_recv, r_send, r_recv,
):
    g = lax.axis_index("grp")
    s = lax.axis_index("lon")
    my_b, my_q = g // NQ, lax.rem(g, NQ)
    core = lax.rem(g, 2)
    sibling = g + 1 - 2 * core
    east, west = lax.rem(s + 1, NS), lax.rem(s + NS - 1, NS)
    mine = pl.ds(g * MB, MB)

    loads = []
    for i, (src, dst) in enumerate(((ens_hbm, ens), (pert_hbm, pert), (ce_hbm, ce), (cn_hbm, cn),
                                    (cell_hbm, cell_ref), (meas_hbm, meas), (var_hbm, var))):
        loads.append(pltpu.make_async_copy(src, dst, load.at[i]))
        loads[-1].start()

    barrier = pltpu.get_barrier_semaphore()
    for i in range(1, NG):
        pl.semaphore_signal(barrier, inc=1, device_id={"grp": lax.rem(g + i, NG)}, device_id_type=MESH)
    for n in (east, west):
        pl.semaphore_signal(barrier, inc=1, device_id={"lon": n}, device_id_type=MESH)

    def remote(src, dst, send, recv, to):
        return pltpu.make_async_remote_copy(
            src_ref=src, dst_ref=dst, send_sem=send, recv_sem=recv, device_id={"grp": to}, device_id_type=MESH)

    def halo(i, to):
        return pltpu.make_async_remote_copy(
            src_ref=hsrc.at[i], dst_ref=hdst.at[i], send_sem=h_send.at[i], recv_sem=h_recv.at[i],
            device_id={"lon": to}, device_id_type=MESH)

    def pert_copy(to, src):
        half = lax.rem(to, 2)
        return remote(pb.at[to // NQ, half], pt.at[half, pl.ds(src * MB, MB)], p_send.at[to], p_recv.at[src], to)

    def pert_pass(src):
        rows = pt.at[core, pl.ds(src * MB, MB)]
        return remote(rows, rows, pf_send.at[src], pf_recv.at[src], sibling)

    def z_copy(to, src):
        half = lax.rem(to, 2)
        return remote(zb.at[to // NQ, half], zr.at[half, pl.ds(src * MB, MB)], z_send.at[to], z_recv.at[src], to)

    def z_pass(src):
        rows = zr.at[core, pl.ds(src * MB, MB)]
        return remote(rows, rows, zf_send.at[src], zf_recv.at[src], sibling)

    def f_copy(to, src):
        return remote(fp.at[to], ft.at[:, pl.ds(src * MB, MB), :], f_send.at[to], f_recv.at[src], to)

    def r_copy(part, to, src):
        x = pl.ds(part * HX, HX)
        return remote(an.at[x, pl.ds(to * MB, MB), :], rb.at[src, x], r_send.at[part, to], r_recv.at[part, src], to)

    def others(body):
        @pl.loop(1, NG)
        def _(i):
            body(lax.rem(g + i, NG))

    for c in loads:
        c.wait()
    hsrc[0] = ens[:, :, LON - 1, :]
    hsrc[1] = ens[:, :, 0, :]
    for b in range(NB):
        for h in range(2):
            pb[b, h] = pert[:, b, h * HO:(h + 1) * HO]
    pl.semaphore_wait(barrier, NG - 1 + 2)
    halo(0, east).start()
    halo(1, west).start()
    others(lambda to: pert_copy(to, g).start())
    for h in range(2):
        pt[h, mine] = pb[my_b, h]

    lane = lax.broadcasted_iota(jnp.int32, (LON, LAT), 1)
    sub = lax.broadcasted_iota(jnp.int32, (LON, LAT), 0)
    for l in range(LEV):
        c = ce[l]
        coef[0, l] = 1.0 - c * c
        coef[1, l] = 0.5 * (c * c - c)
        coef[2, l] = 0.5 * (c * c + c)
        c = cn[l]
        coef[3, l] = 1.0 - c * c
        coef[4, l] = jnp.where(lane == LAT - 1, 0.0, 0.5 * (c * c - c))
        coef[5, l] = jnp.where(lane == 0, 0.0, 0.5 * (c * c + c))

    halo(0, east).wait()
    halo(1, west).wait()

    upper = lane >= 64
    odd = (lane // 32) % 2 == 1
    for q in range(NQ):
        @pl.loop(0, MB, step=UNROLL)
        def _(m0):
            for i in range(UNROLL):
                m = m0 + i
                tiles = []
                for k in range(4):
                    l = 4 * q + k
                    e = ens[m, l]
                    w_edge = jnp.broadcast_to(hdst[0, m, pl.ds(l, 1), :], (LON, LAT))
                    e_edge = jnp.broadcast_to(hdst[1, m, pl.ds(l, 1), :], (LON, LAT))
                    ww = jnp.where(sub == 0, w_edge, pltpu.roll(e, 1, 0))
                    ee = jnp.where(sub == LON - 1, e_edge, pltpu.roll(e, LON - 1, 0))
                    half = coef[0, l] * e + coef[1, l] * ee + coef[2, l] * ww
                    tiles.append(coef[3, l] * half + coef[4, l] * pltpu.roll(half, LAT - 1, 1)
                                 + coef[5, l] * pltpu.roll(half, 1, 1))
                tiles = swap_blocks(tiles, upper, odd)
                for b in range(NB):
                    for x in range(LON):
                        fp[b * NQ + q, x, pl.ds(m, 1), :] = tiles[b][x:x + 1]

    rows = lax.broadcasted_iota(jnp.int32, (LAT, NO), 0)

    @pl.loop(1, NB + 1)
    def _(i):
        b = lax.rem(my_b + i, NB)
        cell = cell_ref[pl.ds(b, 1), :]
        level = cell // (NS * LON * LAT)
        low = (level % 4) * 32 + cell % 32
        high = (level // 4) * LON + (cell // LAT) % LON
        pick = jnp.where(rows == low, 1.0, 0.0).astype(BF16)
        for o in range(0, NO, 256):
            acc = jnp.zeros((MB, 256), F32)
            hi_o = jnp.broadcast_to(high[:, o:o + 256], (MB, 256))
            pk = pick[:, o:o + 256]
            for q in range(NQ):
                f0, f1 = split2(fp[b * NQ + q].reshape(LON * MB, LAT))
                t = jnp.dot(jnp.concatenate([f0, f1], axis=1), jnp.concatenate([pk, pk], axis=0),
                            preferred_element_type=F32)
                for x in range(LON):
                    acc = acc + jnp.where(hi_o == q * LON + x, t[x * MB:(x + 1) * MB], 0.0)
            zb[b, o // HO, :, o % HO:o % HO + 256] = acc

        @pl.loop(0, NQ)
        def _(j):
            to = b * NQ + lax.rem(my_q + j, NQ)

            @pl.when(to != g)
            def _():
                z_copy(to, g).start()

    for h in range(2):
        zr[h, mine] = zb[my_b, h]
    others(lambda to: f_copy(to, g).start())
    ft[:, mine, :] = fp[g]

    def hand_on(arrived, pass_on):
        pass_on(g).start()

        @pl.loop(1, NG)
        def _(i):
            src = lax.rem(g + NG - i, NG)
            arrived(g, src).wait_recv()

            @pl.when(src != sibling)
            def _():
                pass_on(src).start()

    def handed(pass_on):
        others(lambda src: pass_on(src).wait_recv())

    hand_on(pert_copy, pert_pass)
    hand_on(z_copy, z_pass)

    eye = jnp.where(lax.broadcasted_iota(jnp.int32, (M, M), 0) == lax.broadcasted_iota(jnp.int32, (M, M), 1), 1.0, 0.0)
    slot = lax.broadcasted_iota(jnp.int32, (1, HO), 1)
    count = count_ref[my_b]

    def half_sums(h):
        o = pl.ds(pl.multiple_of(h * HO, HO), HO)
        f = zr[h]
        z = (f - jnp.sum(f, axis=0, keepdims=True) * (1.0 / M)) * SCALE
        w = jnp.where(slot + h * HO < count, 1.0 / var[pl.ds(my_b, 1), o], 0.0)
        d = (meas[pl.ds(my_b, 1), o] + pt[h]) - f
        return dot6(jnp.concatenate([z, d], axis=0), z * w, ((1,), (1,)))

    first = half_sums(core)
    mat[...] = first[:M]
    rhs[...] = first[M:]
    handed(pert_pass)
    handed(z_pass)
    second = half_sums(1 - core)
    spread = mat[...] + second[:M]
    mat[...] = spread + eye
    rhs[...] += second[M:]

    low = 1.0 / (jnp.sqrt(jnp.sum(spread * spread)) * 1.0001 + 1.0)
    k = 4.0 / ((1.0 + low) * (1.0 + low))
    inv[...] = (k * low) * ((1.0 + low) * eye - low * mat[...])

    def newton(dot, low):
        k = 4.0 / ((1.0 + low) * (1.0 + low))
        x = inv[...]
        r = (1.0 + low) * eye - dot(mat[...], x)
        inv[...] = k * dot6(x, r)
        return k * low

    low = lax.fori_loop(0, 5, lambda i, low: newton(dot3, low), k * low)
    low = lax.fori_loop(0, 5, lambda i, low: newton(dot6, low), low)
    x = inv[...] * (2.0 / (1.0 + low))
    y = dot3(rhs[...], x)
    for _ in range(2):
        y = y + dot3(rhs[...] - dot6(y, mat[...]), x)
    y0, y1 = split2(y * SCALE)
    lhs = jnp.concatenate([y0, y0, y1], axis=1)

    others(lambda src: f_copy(g, src).wait_recv())
    for part in range(2):
        for x in range(part * HX, (part + 1) * HX, 2):
            f = jnp.concatenate([ft[x], ft[x + 1]], axis=1)
            a0, a1 = split2(f - jnp.sum(f, axis=0, keepdims=True) * (1.0 / M))
            u = f + jnp.dot(lhs, jnp.concatenate([a0, a1, a0], axis=0), preferred_element_type=F32)
            an[x] = u[:, :LAT]
            an[x + 1] = u[:, LAT:]
        others(lambda to: r_copy(part, to, g).start())
    rb[g] = an[:, mine, :]

    def sent(to):
        pert_copy(to, g).wait_send()
        z_copy(to, g).wait_send()
        f_copy(to, g).wait_send()

        @pl.when(to != sibling)
        def _():
            pert_pass(to).wait_send()
            z_pass(to).wait_send()

    others(sent)
    pert_pass(g).wait_send()
    z_pass(g).wait_send()
    for part in range(2):
        others(lambda src: r_copy(part, g, src).wait_recv())

    back = rb.reshape(NG * LON * MB, LAT)
    for q in range(NQ):
        @pl.loop(0, MB, step=8)
        def _(m0):
            for i in range(8):
                m = m0 + i
                tiles = swap_blocks([back[pl.ds((b * NQ + q) * LON * MB + m, LON, stride=MB), :] for b in range(NB)],
                                    upper, odd)
                for k in range(4):
                    out_ref[m, 4 * q + k] = tiles[k]

    for part in range(2):
        others(lambda to: r_copy(part, to, g).wait_send())


def on_device(ensemble, courant_east, northward_courant, measured, error_variance, sensor_cell, sensor_count, perturbation):
    dma = pltpu.SemaphoreType.DMA
    vm = lambda *shape: pltpu.VMEM(shape, F32)
    hbm = pl.BlockSpec(memory_space=pltpu.HBM)
    return pl.pallas_call(
        kernel,
        out_shape=jax.ShapeDtypeStruct((MB, LEV, LON, LAT), F32),
        in_specs=[hbm] * 7 + [pl.BlockSpec(memory_space=pltpu.SMEM)],
        out_specs=pl.BlockSpec(memory_space=pltpu.VMEM),
        scratch_shapes=[
            vm(MB, LEV, LON, LAT), vm(LEV, LON, LAT), vm(LEV, LON, LAT), vm(MB, NB, NO),
            pltpu.VMEM((NB, NO), jnp.int32), vm(NB, NO), vm(NB, NO),
            vm(2, MB, LEV, LAT), vm(2, MB, LEV, LAT), vm(6, LEV, LON, LAT),
            vm(NG, LON, MB, LAT), vm(NB, 2, MB, HO), vm(NB, 2, MB, HO),
            vm(2, M, HO), vm(2, M, HO), vm(LON, M, LAT), vm(LON, M, LAT), vm(NG, LON, MB, LAT),
            vm(M, M), vm(M, M), vm(M, M),
            dma((7,)), dma((2,)), dma((2,)),
        ] + [dma((NG,))] * 10 + [dma((2, NG))] * 2,
        compiler_params=pltpu.CompilerParams(collective_id=0, has_side_effects=True, vmem_limit_bytes=62 << 20),
    )(ensemble, courant_east, northward_courant, perturbation, sensor_cell, measured, error_variance, sensor_count)


def solution(mesh):
    return jax.shard_map(
        on_device,
        mesh=mesh,
        in_specs=(
            P("grp", None, "lon", None),
            P(None, "lon", None),
            P(None, "lon", None),
            P("lon", None),
            P("lon", None),
            P("lon", None),
            P("lon"),
            P("grp", "lon", None),
        ),
        out_specs=P("grp", None, "lon", None),
        check_vma=False,
    )
```

time: 517 us -> 75.7 us (0.15)
  the two profiles are of different devices: /device:TPU:1 before, /device:TPU:5 now
where the time goes in v2:
time: 75.7 us; the launch traced here: 75.5 us
  Pallas kernels  73.2 us (97%)
  local copies, waits for them, and re-layouts  2.3 us (3%)
    pallas_call x1, Pallas kernels, on_device(): pl.pallas_call(kernel, out_shape=jax.ShapeDtypeStruct((MB, LEV, LON, LAT)...  73.2 us
    unnamed x1, local copies, waits for them, and re-layouts  2.3 us

profile of v2, /device:TPU:5, one launch (start us, length us, event | category | flops | bytes accessed | tf_op | source)
XLA Modules:
  0.0 75.5 jit_solution(17518057401527027537)
XLA Ops:
  0.0 73.2 %shard_map.82 = f32[16,16,8,128]{3,2,1,0:T(8,128)} custom-call(f32[16,16,8,128]{3,2,1,0:T(8,128)} %ens_hbm.1, f32[16,8,128]{2,1,0:T(8,128)} %ce_hbm.1, f32[16,8,128]{2,1,0:T(8,128)} %cn_hbm.1, f32[16,4,1024]{2,1,0:T(4,128)} %pert_hbm.1, s32[4,1024]{1,0:T(4,128)} %cell_hbm.1, f32[4,1024]{1,0:T(4,128)} %meas_hbm.1, f32[4,1024]{1,0:T(4,128)} %var_hbm.1, s32[4]{0:T(128)} %count_ref.1), custom_call_target="tpu_custom_call" | custom-call | tf_op jit(solution)/shard_map/pallas_call | solution.py:316
  73.2 2.3 %copy.10 = f32[16,16,8,128]{3,2,1,0:T(8,128)} copy(f32[16,16,8,128]{3,2,1,0:T(8,128)} %shard_map.82) | data formatting | bytes 2097152

commit v3 on v2

--- a/solution.py
+++ b/solution.py
@@ -25,12 +25,18 @@
 HX = LON // 2
 SCALE = 1.0 / math.sqrt(M - 1)
 UNROLL = 4
+NR = NG // 2
+MR = NR * MB
 
 
 def split2(x):
     hi = x.astype(BF16)
     lo = (x - hi.astype(F32)).astype(BF16)
     return hi, lo
+
+
+def device_of(b, q):
+    return (q // 2) * NR + b * 2 + q % 2
 
 
 def dot6(a, b, dims=((1,), (0,))):
@@ -61,12 +67,12 @@
     out_ref,
     ens, ce, cn, pert, cell_ref, meas, var, hsrc, hdst, coef, fp, zb, pb, zr, pt, ft, an, rb, mat, rhs, inv,
     load, h_send, h_recv, p_send, p_recv, pf_send, pf_recv, z_send, z_recv, zf_send, zf_recv,
-    f_send, f_recv, r_send, r_recv,
+    f_send, f_recv, r_send, r_recv, x_send, x_recv,
 ):
     g = lax.axis_index("grp")
     s = lax.axis_index("lon")
-    my_b, my_q = g // NQ, lax.rem(g, NQ)
-    core = lax.rem(g, 2)
+    row, my_b, core = g // NR, lax.rem(g, NR) // 2, lax.rem(g, 2)
+    partner = lax.rem(g + NR, NG)
     sibling = g + 1 - 2 * core
     east, west = lax.rem(s + 1, NS), lax.rem(s + NS - 1, NS)
     mine = pl.ds(g * MB, MB)
@@ -87,22 +93,24 @@
         return pltpu.make_async_remote_copy(
             src_ref=src, dst_ref=dst, send_sem=send, recv_sem=recv, device_id={"grp": to}, device_id_type=MESH)
 
-    def halo(i, to):
+    def halo(i, c, to):
+        rows = pl.ds(c * UNROLL, UNROLL)
         return pltpu.make_async_remote_copy(
-            src_ref=hsrc.at[i], dst_ref=hdst.at[i], send_sem=h_send.at[i], recv_sem=h_recv.at[i],
+            src_ref=hsrc.at[i, rows], dst_ref=hdst.at[i, rows], send_sem=h_send.at[i, c], recv_sem=h_recv.at[i, c],
             device_id={"lon": to}, device_id_type=MESH)
 
     def pert_copy(to, src):
         half = lax.rem(to, 2)
-        return remote(pb.at[to // NQ, half], pt.at[half, pl.ds(src * MB, MB)], p_send.at[to], p_recv.at[src], to)
+        return remote(pb.at[lax.rem(to, NR) // 2, half], pt.at[half, pl.ds(lax.rem(src, NR) * MB, MB)],
+                      p_send.at[to], p_recv.at[src], to)
 
     def pert_pass(src):
-        rows = pt.at[core, pl.ds(src * MB, MB)]
+        rows = pt.at[core, pl.ds(lax.rem(src, NR) * MB, MB)]
         return remote(rows, rows, pf_send.at[src], pf_recv.at[src], sibling)
 
     def z_copy(to, src):
         half = lax.rem(to, 2)
-        return remote(zb.at[to // NQ, half], zr.at[half, pl.ds(src * MB, MB)], z_send.at[to], z_recv.at[src], to)
+        return remote(zb.at[lax.rem(to, NR) // 2, half], zr.at[half, pl.ds(src * MB, MB)], z_send.at[to], z_recv.at[src], to)
 
     def z_pass(src):
         rows = zr.at[core, pl.ds(src * MB, MB)]
@@ -115,10 +123,30 @@
         x = pl.ds(part * HX, HX)
         return remote(an.at[x, pl.ds(to * MB, MB), :], rb.at[src, x], r_send.at[part, to], r_recv.at[part, src], to)
 
-    def others(body):
-        @pl.loop(1, NG)
+    def rhs_copy(to_row):
+        rows = rhs.at[pl.ds((1 - to_row) * MR + core * (MR // 2), MR // 2)]
+        return remote(rows, rows, x_send.at[0], x_recv.at[0], partner)
+
+    def rhs_pass(half):
+        rows = rhs.at[pl.ds((1 - row) * MR + half * (MR // 2), MR // 2)]
+        return remote(rows, rows, x_send.at[1], x_recv.at[1], sibling)
+
+    def stepped(i, dy, sign):
+        k = i // 4
+        dx = lax.rem(1 + 2 * k + k // 2, 4)
+        x = lax.rem(my_b + 4 + sign * dx, 4)
+        dc = 1 - lax.rem(i, 4) // 2
+        return lax.rem(row + dy, 2) * NR + x * 2 + lax.rem(core + dc, 2)
+
+    def same_row(body, sign=1):
+        @pl.loop(0, NR - 1)
         def _(i):
-            body(lax.rem(g + i, NG))
+            body(stepped(2 * i, 0, sign))
+
+    def others(body, sign=1, first=0, last=NG - 1):
+        @pl.loop(first, last)
+        def _(i):
+            body(stepped(i, 1 - lax.rem(i, 2), sign))
 
     for c in loads:
         c.wait()
@@ -128,11 +156,15 @@
         for h in range(2):
             pb[b, h] = pert[:, b, h * HO:(h + 1) * HO]
     pl.semaphore_wait(barrier, NG - 1 + 2)
-    halo(0, east).start()
-    halo(1, west).start()
-    others(lambda to: pert_copy(to, g).start())
+
+    @pl.loop(0, MB // UNROLL)
+    def _(c):
+        halo(0, c, east).start()
+        halo(1, c, west).start()
+
+    same_row(lambda to: pert_copy(to, g).start())
     for h in range(2):
-        pt[h, mine] = pb[my_b, h]
+        pt[h, pl.ds(lax.rem(g, NR) * MB, MB)] = pb[my_b, h]
 
     lane = lax.broadcasted_iota(jnp.int32, (LON, LAT), 1)
     sub = lax.broadcasted_iota(jnp.int32, (LON, LAT), 0)
@@ -146,16 +178,17 @@
         coef[4, l] = jnp.where(lane == LAT - 1, 0.0, 0.5 * (c * c - c))
         coef[5, l] = jnp.where(lane == 0, 0.0, 0.5 * (c * c + c))
 
-    halo(0, east).wait()
-    halo(1, west).wait()
 
     upper = lane >= 64
     odd = (lane // 32) % 2 == 1
-    for q in range(NQ):
-        @pl.loop(0, MB, step=UNROLL)
-        def _(m0):
+
+    @pl.loop(0, MB // UNROLL)
+    def _(c):
+        halo(0, c, east).wait()
+        halo(1, c, west).wait()
+        for q in range(NQ):
             for i in range(UNROLL):
-                m = m0 + i
+                m = c * UNROLL + i
                 tiles = []
                 for k in range(4):
                     l = 4 * q + k
@@ -170,13 +203,13 @@
                 tiles = swap_blocks(tiles, upper, odd)
                 for b in range(NB):
                     for x in range(LON):
-                        fp[b * NQ + q, x, pl.ds(m, 1), :] = tiles[b][x:x + 1]
+                        fp[device_of(b, q), x, pl.ds(m, 1), :] = tiles[b][x:x + 1]
 
     rows = lax.broadcasted_iota(jnp.int32, (LAT, NO), 0)
 
-    @pl.loop(1, NB + 1)
-    def _(i):
-        b = lax.rem(my_b + i, NB)
+    @pl.loop(0, NB)
+    def _(k):
+        b = lax.rem(my_b + lax.rem(1 + 2 * k + k // 2, 4), NB)
         cell = cell_ref[pl.ds(b, 1), :]
         level = cell // (NS * LON * LAT)
         low = (level % 4) * 32 + cell % 32
@@ -187,7 +220,7 @@
             hi_o = jnp.broadcast_to(high[:, o:o + 256], (MB, 256))
             pk = pick[:, o:o + 256]
             for q in range(NQ):
-                f0, f1 = split2(fp[b * NQ + q].reshape(LON * MB, LAT))
+                f0, f1 = split2(fp[device_of(b, q)].reshape(LON * MB, LAT))
                 t = jnp.dot(jnp.concatenate([f0, f1], axis=1), jnp.concatenate([pk, pk], axis=0),
                             preferred_element_type=F32)
                 for x in range(LON):
@@ -196,7 +229,7 @@
 
         @pl.loop(0, NQ)
         def _(j):
-            to = b * NQ + lax.rem(my_q + j, NQ)
+            to = stepped(4 * k + j, 1 - lax.rem(j, 2), 1)
 
             @pl.when(to != g)
             def _():
@@ -204,48 +237,48 @@
 
     for h in range(2):
         zr[h, mine] = zb[my_b, h]
-    others(lambda to: f_copy(to, g).start())
-    ft[:, mine, :] = fp[g]
-
-    def hand_on(arrived, pass_on):
+
+    def hand_on(sources, arrived, pass_on):
         pass_on(g).start()
 
-        @pl.loop(1, NG)
-        def _(i):
-            src = lax.rem(g + NG - i, NG)
+        def arrive(src):
             arrived(g, src).wait_recv()
 
             @pl.when(src != sibling)
             def _():
                 pass_on(src).start()
 
-    def handed(pass_on):
-        others(lambda src: pass_on(src).wait_recv())
-
-    hand_on(pert_copy, pert_pass)
-    hand_on(z_copy, z_pass)
+        sources(arrive, -1)
+
+    hand_on(same_row, pert_copy, pert_pass)
+    hand_on(others, z_copy, z_pass)
+    others(lambda to: f_copy(to, g).start(), last=8)
+    ft[:, mine, :] = fp[g]
 
     eye = jnp.where(lax.broadcasted_iota(jnp.int32, (M, M), 0) == lax.broadcasted_iota(jnp.int32, (M, M), 1), 1.0, 0.0)
     slot = lax.broadcasted_iota(jnp.int32, (1, HO), 1)
     count = count_ref[my_b]
+    row_rows = pl.ds(row * MR, MR)
 
     def half_sums(h):
         o = pl.ds(pl.multiple_of(h * HO, HO), HO)
         f = zr[h]
         z = (f - jnp.sum(f, axis=0, keepdims=True) * (1.0 / M)) * SCALE
         w = jnp.where(slot + h * HO < count, 1.0 / var[pl.ds(my_b, 1), o], 0.0)
-        d = (meas[pl.ds(my_b, 1), o] + pt[h]) - f
+        d = (meas[pl.ds(my_b, 1), o] + pt[h]) - zr[h, row_rows]
         return dot6(jnp.concatenate([z, d], axis=0), z * w, ((1,), (1,)))
 
     first = half_sums(core)
     mat[...] = first[:M]
-    rhs[...] = first[M:]
-    handed(pert_pass)
-    handed(z_pass)
+    rhs[row_rows] = first[M:]
+    same_row(lambda src: pert_pass(src).wait_recv())
+    others(lambda src: z_pass(src).wait_recv())
     second = half_sums(1 - core)
     spread = mat[...] + second[:M]
     mat[...] = spread + eye
-    rhs[...] += second[M:]
+    rhs[row_rows] += second[M:]
+    rhs_copy(1 - row).start()
+    others(lambda to: f_copy(to, g).start(), first=8)
 
     low = 1.0 / (jnp.sqrt(jnp.sum(spread * spread)) * 1.0001 + 1.0)
     k = 4.0 / ((1.0 + low) * (1.0 + low))
@@ -259,8 +292,12 @@
         return k * low
 
     low = lax.fori_loop(0, 5, lambda i, low: newton(dot3, low), k * low)
-    low = lax.fori_loop(0, 5, lambda i, low: newton(dot6, low), low)
+    low = lax.fori_loop(0, 4, lambda i, low: newton(dot6, low), low)
+    rhs_copy(row).wait_recv()
+    rhs_pass(core).start()
+    low = newton(dot6, low)
     x = inv[...] * (2.0 / (1.0 + low))
+    rhs_pass(1 - core).wait_recv()
     y = dot3(rhs[...], x)
     for _ in range(2):
         y = y + dot3(rhs[...] - dot6(y, mat[...]), x)
@@ -279,16 +316,24 @@
     rb[g] = an[:, mine, :]
 
     def sent(to):
-        pert_copy(to, g).wait_send()
         z_copy(to, g).wait_send()
         f_copy(to, g).wait_send()
+
+        @pl.when(to != sibling)
+        def _():
+            z_pass(to).wait_send()
+
+    def pert_sent(to):
+        pert_copy(to, g).wait_send()
 
         @pl.when(to != sibling)
         def _():
             pert_pass(to).wait_send()
-            z_pass(to).wait_send()
 
     others(sent)
+    same_row(pert_sent)
+    rhs_copy(1 - row).wait_send()
+    rhs_pass(core).wait_send()
     pert_pass(g).wait_send()
     z_pass(g).wait_send()
     for part in range(2):
@@ -300,7 +345,7 @@
         def _(m0):
             for i in range(8):
                 m = m0 + i
-                tiles = swap_blocks([back[pl.ds((b * NQ + q) * LON * MB + m, LON, stride=MB), :] for b in range(NB)],
+                tiles = swap_blocks([back[pl.ds(device_of(b, q) * LON * MB + m, LON, stride=MB), :] for b in range(NB)],
                                     upper, odd)
                 for k in range(4):
                     out_ref[m, 4 * q + k] = tiles[k]
@@ -323,10 +368,10 @@
             pltpu.VMEM((NB, NO), jnp.int32), vm(NB, NO), vm(NB, NO),
             vm(2, MB, LEV, LAT), vm(2, MB, LEV, LAT), vm(6, LEV, LON, LAT),
             vm(NG, LON, MB, LAT), vm(NB, 2, MB, HO), vm(NB, 2, MB, HO),
-            vm(2, M, HO), vm(2, M, HO), vm(LON, M, LAT), vm(LON, M, LAT), vm(NG, LON, MB, LAT),
+            vm(2, M, HO), vm(2, MR, HO), vm(LON, M, LAT), vm(LON, M, LAT), vm(NG, LON, MB, LAT),
             vm(M, M), vm(M, M), vm(M, M),
-            dma((7,)), dma((2,)), dma((2,)),
-        ] + [dma((NG,))] * 10 + [dma((2, NG))] * 2,
+            dma((7,)), dma((2, MB // UNROLL)), dma((2, MB // UNROLL)),
+        ] + [dma((NG,))] * 10 + [dma((2, NG))] * 2 + [dma((2,))] * 2,
         compiler_params=pltpu.CompilerParams(collective_id=0, has_side_effects=True, vmem_limit_bytes=62 << 20),
     )(ensemble, courant_east, northward_courant, perturbation, sensor_cell, measured, error_variance, sensor_count)
 

time: 75.7 us -> 65.1 us (0.86)
  the two profiles are of different devices: /device:TPU:5 before, /device:TPU:1 now
where the time goes in v3:
time: 65.1 us; the launch traced here: 65 us
  Pallas kernels  62.7 us (96%)
  local copies, waits for them, and re-layouts  2.3 us (4%)
    pallas_call x1, Pallas kernels, on_device(): pl.pallas_call(kernel, out_shape=jax.ShapeDtypeStruct((MB, LEV, LON, LAT)...  62.7 us
    unnamed x1, local copies, waits for them, and re-layouts  2.3 us

profile of v3, /device:TPU:1, one launch (start us, length us, event | category | flops | bytes accessed | tf_op | source)
XLA Modules:
  0.0 65.0 jit_solution(14983245774071268705)
XLA Ops:
  0.0 62.7 %shard_map.82 = f32[16,16,8,128]{3,2,1,0:T(8,128)} custom-call(f32[16,16,8,128]{3,2,1,0:T(8,128)} %ens_hbm.1, f32[16,8,128]{2,1,0:T(8,128)} %ce_hbm.1, f32[16,8,128]{2,1,0:T(8,128)} %cn_hbm.1, f32[16,4,1024]{2,1,0:T(4,128)} %pert_hbm.1, s32[4,1024]{1,0:T(4,128)} %cell_hbm.1, f32[4,1024]{1,0:T(4,128)} %meas_hbm.1, f32[4,1024]{1,0:T(4,128)} %var_hbm.1, s32[4]{0:T(128)} %count_ref.1), custom_call_target="tpu_custom_call" | custom-call | tf_op jit(solution)/shard_map/pallas_call | solution.py:361
  62.7 2.3 %copy.10 = f32[16,16,8,128]{3,2,1,0:T(8,128)} copy(f32[16,16,8,128]{3,2,1,0:T(8,128)} %shard_map.82) | data formatting | bytes 2097152

commit v4 on v3

--- a/solution.py
+++ b/solution.py
@@ -43,6 +43,33 @@
     return lax.dot_general(a, b, (dims, ((), ())), precision=lax.Precision.HIGHEST, preferred_element_type=F32)
 
 
+def split3(x):
+    x0 = x.astype(BF16)
+    rest = x - x0.astype(F32)
+    x1, x2 = split2(rest)
+    return x0, x1, x2
+
+
+def left3(p):
+    return jnp.concatenate([p[0], p[0], p[1]], axis=1)
+
+
+def right3(p):
+    return jnp.concatenate([p[0], p[1], p[0]], axis=0)
+
+
+def left6(p):
+    return jnp.concatenate([p[0], p[0], p[0], p[1], p[1], p[2]], axis=1)
+
+
+def right6(p):
+    return jnp.concatenate([p[0], p[1], p[2], p[0], p[1], p[0]], axis=0)
+
+
+def mul(a, b):
+    return jnp.dot(a, b, preferred_element_type=F32)
+
+
 def dot3(a, b):
     a0, a1 = split2(a)
     b0, b1 = split2(b)
@@ -64,10 +91,10 @@
 
 def kernel(
     ens_hbm, ce_hbm, cn_hbm, pert_hbm, cell_hbm, meas_hbm, var_hbm, count_ref,
-    out_ref,
-    ens, ce, cn, pert, cell_ref, meas, var, hsrc, hdst, coef, fp, zb, pb, zr, pt, ft, an, rb, mat, rhs, inv,
-    load, h_send, h_recv, p_send, p_recv, pf_send, pf_recv, z_send, z_recv, zf_send, zf_recv,
-    f_send, f_recv, r_send, r_recv, x_send, x_recv,
+    rb,
+    ens, ce, cn, pert, cell_ref, meas, var, hsrc, hdst, coef, fp, zb, pb, zr, pt, ft, an, mat, rhs, inv, mp, own_sums, other_sums,
+    load, h_send, h_recv, p_send, p_recv, z_send, z_recv,
+    f_send, f_recv, r_send, r_recv, x_send, x_recv, s_send, s_recv,
 ):
     g = lax.axis_index("grp")
     s = lax.axis_index("lon")
@@ -77,18 +104,18 @@
     east, west = lax.rem(s + 1, NS), lax.rem(s + NS - 1, NS)
     mine = pl.ds(g * MB, MB)
 
+    barrier = pltpu.get_barrier_semaphore()
+    for i in range(1, NG):
+        pl.semaphore_signal(barrier, inc=1, device_id={"grp": lax.rem(g + i, NG)}, device_id_type=MESH)
+    for n in (east, west):
+        pl.semaphore_signal(barrier, inc=1, device_id={"lon": n}, device_id_type=MESH)
+
     loads = []
     for i, (src, dst) in enumerate(((ens_hbm, ens), (pert_hbm, pert), (ce_hbm, ce), (cn_hbm, cn),
                                     (cell_hbm, cell_ref), (meas_hbm, meas), (var_hbm, var))):
         loads.append(pltpu.make_async_copy(src, dst, load.at[i]))
         loads[-1].start()
 
-    barrier = pltpu.get_barrier_semaphore()
-    for i in range(1, NG):
-        pl.semaphore_signal(barrier, inc=1, device_id={"grp": lax.rem(g + i, NG)}, device_id_type=MESH)
-    for n in (east, west):
-        pl.semaphore_signal(barrier, inc=1, device_id={"lon": n}, device_id_type=MESH)
-
     def remote(src, dst, send, recv, to):
         return pltpu.make_async_remote_copy(
             src_ref=src, dst_ref=dst, send_sem=send, recv_sem=recv, device_id={"grp": to}, device_id_type=MESH)
@@ -101,20 +128,16 @@
 
     def pert_copy(to, src):
         half = lax.rem(to, 2)
-        return remote(pb.at[lax.rem(to, NR) // 2, half], pt.at[half, pl.ds(lax.rem(src, NR) * MB, MB)],
+        return remote(pb.at[lax.rem(to, NR) // 2, half], pt.at[pl.ds(lax.rem(src, NR) * MB, MB)],
                       p_send.at[to], p_recv.at[src], to)
-
-    def pert_pass(src):
-        rows = pt.at[core, pl.ds(lax.rem(src, NR) * MB, MB)]
-        return remote(rows, rows, pf_send.at[src], pf_recv.at[src], sibling)
 
     def z_copy(to, src):
         half = lax.rem(to, 2)
-        return remote(zb.at[lax.rem(to, NR) // 2, half], zr.at[half, pl.ds(src * MB, MB)], z_send.at[to], z_recv.at[src], to)
-
-    def z_pass(src):
-        rows = zr.at[core, pl.ds(src * MB, MB)]
-        return remote(rows, rows, zf_send.at[src], zf_recv.at[src], sibling)
+        return remote(zb.at[lax.rem(to, NR) // 2, half], zr.at[pl.ds(src * MB, MB)], z_send.at[to], z_recv.at[src], to)
+
+    def sums_copy(i):
+        rows = pl.ds(i * M, M if i == 0 else MR)
+        return remote(own_sums.at[rows], other_sums.at[rows], s_send.at[i], s_recv.at[i], sibling)
 
     def f_copy(to, src):
         return remote(fp.at[to], ft.at[:, pl.ds(src * MB, MB), :], f_send.at[to], f_recv.at[src], to)
@@ -133,28 +156,24 @@
 
     def stepped(i, dy, sign):
         k = i // 4
-        dx = lax.rem(1 + 2 * k + k // 2, 4)
+        dx = (1 + 2 * k + k // 2) % 4
         x = lax.rem(my_b + 4 + sign * dx, 4)
-        dc = 1 - lax.rem(i, 4) // 2
+        dc = 1 - i % 4 // 2
         return lax.rem(row + dy, 2) * NR + x * 2 + lax.rem(core + dc, 2)
 
+    order = {sign: [stepped(i, 1 - i % 2, sign) for i in range(NG)] for sign in (1, -1)}
+
     def same_row(body, sign=1):
-        @pl.loop(0, NR - 1)
-        def _(i):
-            body(stepped(2 * i, 0, sign))
+        for i in range(NR - 1):
+            body(order[sign][2 * i + 1])
 
     def others(body, sign=1, first=0, last=NG - 1):
-        @pl.loop(first, last)
-        def _(i):
-            body(stepped(i, 1 - lax.rem(i, 2), sign))
-
-    for c in loads:
-        c.wait()
+        for i in range(first, last):
+            body(order[sign][i])
+
+    loads[0].wait()
     hsrc[0] = ens[:, :, LON - 1, :]
     hsrc[1] = ens[:, :, 0, :]
-    for b in range(NB):
-        for h in range(2):
-            pb[b, h] = pert[:, b, h * HO:(h + 1) * HO]
     pl.semaphore_wait(barrier, NG - 1 + 2)
 
     @pl.loop(0, MB // UNROLL)
@@ -162,9 +181,13 @@
         halo(0, c, east).start()
         halo(1, c, west).start()
 
+    for c in loads[1:]:
+        c.wait()
+    for b in range(NB):
+        for h in range(2):
+            pb[b, h] = pert[:, b, h * HO:(h + 1) * HO]
     same_row(lambda to: pert_copy(to, g).start())
-    for h in range(2):
-        pt[h, pl.ds(lax.rem(g, NR) * MB, MB)] = pb[my_b, h]
+    pt[pl.ds(lax.rem(g, NR) * MB, MB)] = pb[my_b, core]
 
     lane = lax.broadcasted_iota(jnp.int32, (LON, LAT), 1)
     sub = lax.broadcasted_iota(jnp.int32, (LON, LAT), 0)
@@ -207,9 +230,8 @@
 
     rows = lax.broadcasted_iota(jnp.int32, (LAT, NO), 0)
 
-    @pl.loop(0, NB)
-    def _(k):
-        b = lax.rem(my_b + lax.rem(1 + 2 * k + k // 2, 4), NB)
+    for k in range(NB):
+        b = lax.rem(my_b + (1 + 2 * k + k // 2) % 4, NB)
         cell = cell_ref[pl.ds(b, 1), :]
         level = cell // (NS * LON * LAT)
         low = (level % 4) * 32 + cell % 32
@@ -227,31 +249,14 @@
                     acc = acc + jnp.where(hi_o == q * LON + x, t[x * MB:(x + 1) * MB], 0.0)
             zb[b, o // HO, :, o % HO:o % HO + 256] = acc
 
-        @pl.loop(0, NQ)
-        def _(j):
-            to = stepped(4 * k + j, 1 - lax.rem(j, 2), 1)
-
-            @pl.when(to != g)
-            def _():
-                z_copy(to, g).start()
-
-    for h in range(2):
-        zr[h, mine] = zb[my_b, h]
-
-    def hand_on(sources, arrived, pass_on):
-        pass_on(g).start()
-
-        def arrive(src):
-            arrived(g, src).wait_recv()
-
-            @pl.when(src != sibling)
-            def _():
-                pass_on(src).start()
-
-        sources(arrive, -1)
-
-    hand_on(same_row, pert_copy, pert_pass)
-    hand_on(others, z_copy, z_pass)
+        for j in range(NQ):
+            if 4 * k + j < NG - 1:
+                z_copy(order[1][4 * k + j], g).start()
+
+    zr[mine] = zb[my_b, core]
+
+    same_row(lambda src: pert_copy(g, src).wait_recv(), -1)
+    others(lambda src: z_copy(g, src).wait_recv(), -1)
     others(lambda to: f_copy(to, g).start(), last=8)
     ft[:, mine, :] = fp[g]
 
@@ -260,47 +265,49 @@
     count = count_ref[my_b]
     row_rows = pl.ds(row * MR, MR)
 
-    def half_sums(h):
-        o = pl.ds(pl.multiple_of(h * HO, HO), HO)
-        f = zr[h]
-        z = (f - jnp.sum(f, axis=0, keepdims=True) * (1.0 / M)) * SCALE
-        w = jnp.where(slot + h * HO < count, 1.0 / var[pl.ds(my_b, 1), o], 0.0)
-        d = (meas[pl.ds(my_b, 1), o] + pt[h]) - zr[h, row_rows]
-        return dot6(jnp.concatenate([z, d], axis=0), z * w, ((1,), (1,)))
-
-    first = half_sums(core)
-    mat[...] = first[:M]
-    rhs[row_rows] = first[M:]
-    same_row(lambda src: pert_pass(src).wait_recv())
-    others(lambda src: z_pass(src).wait_recv())
-    second = half_sums(1 - core)
-    spread = mat[...] + second[:M]
+    o = pl.ds(pl.multiple_of(core * HO, HO), HO)
+    f = zr[...]
+    z = (f - jnp.sum(f, axis=0, keepdims=True) * (1.0 / M)) * SCALE
+    zw = z * jnp.where(slot + core * HO < count, 1.0 / var[pl.ds(my_b, 1), o], 0.0)
+    own_sums[:M] = dot6(z, zw, ((1,), (1,)))
+    sums_copy(0).start()
+    d = (meas[pl.ds(my_b, 1), o] + pt[...]) - zr[row_rows]
+    own_sums[M:] = dot6(d, zw, ((1,), (1,)))
+    sums_copy(1).start()
+    sums_copy(0).wait_recv()
+    spread = own_sums[:M] + other_sums[:M]
     mat[...] = spread + eye
-    rhs[row_rows] += second[M:]
-    rhs_copy(1 - row).start()
-    others(lambda to: f_copy(to, g).start(), first=8)
 
     low = 1.0 / (jnp.sqrt(jnp.sum(spread * spread)) * 1.0001 + 1.0)
     k = 4.0 / ((1.0 + low) * (1.0 + low))
     inv[...] = (k * low) * ((1.0 + low) * eye - low * mat[...])
 
-    def newton(dot, low):
+    pieces = split3(mat[...])
+    for i in range(3):
+        mp[:, i * M:(i + 1) * M] = pieces[i]
+
+    def newton(exact, low):
         k = 4.0 / ((1.0 + low) * (1.0 + low))
-        x = inv[...]
-        r = (1.0 + low) * eye - dot(mat[...], x)
-        inv[...] = k * dot6(x, r)
+        m = [mp[:, i * M:(i + 1) * M] for i in range(3)]
+        x = split3(inv[...])
+        r = (1.0 + low) * eye - (mul(left6(x), right6(m)) if exact else mul(left3(x), right3(m)))
+        inv[...] = k * mul(left6(split3(r)), right6(x))
         return k * low
 
-    low = lax.fori_loop(0, 5, lambda i, low: newton(dot3, low), k * low)
-    low = lax.fori_loop(0, 4, lambda i, low: newton(dot6, low), low)
+    sums_copy(1).wait_recv()
+    rhs[row_rows] = own_sums[M:] + other_sums[M:]
+    rhs_copy(1 - row).start()
+    others(lambda to: f_copy(to, g).start(), first=8)
+    low = lax.fori_loop(0, 7, lambda i, low: newton(False, low), k * low)
+    low = lax.fori_loop(0, 3, lambda i, low: newton(True, low), low)
     rhs_copy(row).wait_recv()
     rhs_pass(core).start()
-    low = newton(dot6, low)
-    x = inv[...] * (2.0 / (1.0 + low))
+    x = right3(split2(inv[...] * (2.0 / (1.0 + low))))
     rhs_pass(1 - core).wait_recv()
-    y = dot3(rhs[...], x)
+    m = right6([mp[:, i * M:(i + 1) * M] for i in range(3)])
+    y = mul(left3(split2(rhs[...])), x)
     for _ in range(2):
-        y = y + dot3(rhs[...] - dot6(y, mat[...]), x)
+        y = y + mul(left3(split2(rhs[...] - mul(left6(split3(y)), m))), x)
     y0, y1 = split2(y * SCALE)
     lhs = jnp.concatenate([y0, y0, y1], axis=1)
 
@@ -313,67 +320,87 @@
             an[x] = u[:, :LAT]
             an[x + 1] = u[:, LAT:]
         others(lambda to: r_copy(part, to, g).start())
-    rb[g] = an[:, mine, :]
+    own = pltpu.make_async_copy(an.at[:, mine, :], rb.at[g], load.at[0])
+    own.start()
 
     def sent(to):
         z_copy(to, g).wait_send()
         f_copy(to, g).wait_send()
 
-        @pl.when(to != sibling)
-        def _():
-            z_pass(to).wait_send()
-
-    def pert_sent(to):
-        pert_copy(to, g).wait_send()
-
-        @pl.when(to != sibling)
-        def _():
-            pert_pass(to).wait_send()
-
     others(sent)
-    same_row(pert_sent)
+    same_row(lambda to: pert_copy(to, g).wait_send())
+    for i in range(2):
+        sums_copy(i).wait_send()
     rhs_copy(1 - row).wait_send()
     rhs_pass(core).wait_send()
-    pert_pass(g).wait_send()
-    z_pass(g).wait_send()
     for part in range(2):
         others(lambda src: r_copy(part, g, src).wait_recv())
 
-    back = rb.reshape(NG * LON * MB, LAT)
+    for part in range(2):
+        others(lambda to: r_copy(part, to, g).wait_send())
+    own.wait()
+
+
+def unpack_kernel(rb, out_hbm, buf, out, loaded, stored):
+    lane = lax.broadcasted_iota(jnp.int32, (LON, LAT), 1)
+    upper = lane >= 64
+    odd = (lane // 32) % 2 == 1
+
+    def load(q):
+        return pltpu.make_async_copy(rb.at[q // 2, :, q % 2], buf.at[q], loaded.at[q])
+
+    def store(q):
+        levels = pl.ds(q * (LEV // NQ), LEV // NQ)
+        return pltpu.make_async_copy(out.at[:, levels], out_hbm.at[:, levels], stored.at[q])
+
     for q in range(NQ):
+        load(q).start()
+    back = buf.reshape(NQ * NB * LON * MB, LAT)
+    for q in range(NQ):
+        load(q).wait()
+
         @pl.loop(0, MB, step=8)
         def _(m0):
             for i in range(8):
                 m = m0 + i
-                tiles = swap_blocks([back[pl.ds(device_of(b, q) * LON * MB + m, LON, stride=MB), :] for b in range(NB)],
+                tiles = swap_blocks([back[pl.ds((q * NB + b) * LON * MB + m, LON, stride=MB), :] for b in range(NB)],
                                     upper, odd)
                 for k in range(4):
-                    out_ref[m, 4 * q + k] = tiles[k]
-
-    for part in range(2):
-        others(lambda to: r_copy(part, to, g).wait_send())
+                    out[m, 4 * q + k] = tiles[k]
+
+        store(q).start()
+    for q in range(NQ):
+        store(q).wait()
 
 
 def on_device(ensemble, courant_east, northward_courant, measured, error_variance, sensor_cell, sensor_count, perturbation):
     dma = pltpu.SemaphoreType.DMA
     vm = lambda *shape: pltpu.VMEM(shape, F32)
     hbm = pl.BlockSpec(memory_space=pltpu.HBM)
-    return pl.pallas_call(
+    back = pl.pallas_call(
         kernel,
-        out_shape=jax.ShapeDtypeStruct((MB, LEV, LON, LAT), F32),
+        out_shape=jax.ShapeDtypeStruct((NG, LON, MB, LAT), F32),
         in_specs=[hbm] * 7 + [pl.BlockSpec(memory_space=pltpu.SMEM)],
-        out_specs=pl.BlockSpec(memory_space=pltpu.VMEM),
+        out_specs=hbm,
         scratch_shapes=[
             vm(MB, LEV, LON, LAT), vm(LEV, LON, LAT), vm(LEV, LON, LAT), vm(MB, NB, NO),
             pltpu.VMEM((NB, NO), jnp.int32), vm(NB, NO), vm(NB, NO),
             vm(2, MB, LEV, LAT), vm(2, MB, LEV, LAT), vm(6, LEV, LON, LAT),
             vm(NG, LON, MB, LAT), vm(NB, 2, MB, HO), vm(NB, 2, MB, HO),
-            vm(2, M, HO), vm(2, MR, HO), vm(LON, M, LAT), vm(LON, M, LAT), vm(NG, LON, MB, LAT),
-            vm(M, M), vm(M, M), vm(M, M),
+            vm(M, HO), vm(MR, HO), vm(LON, M, LAT), vm(LON, M, LAT),
+            vm(M, M), vm(M, M), vm(M, M), pltpu.VMEM((M, 3 * M), BF16), vm(M + MR, M), vm(M + MR, M),
             dma((7,)), dma((2, MB // UNROLL)), dma((2, MB // UNROLL)),
-        ] + [dma((NG,))] * 10 + [dma((2, NG))] * 2 + [dma((2,))] * 2,
+        ] + [dma((NG,))] * 6 + [dma((2, NG))] * 2 + [dma((2,))] * 4,
         compiler_params=pltpu.CompilerParams(collective_id=0, has_side_effects=True, vmem_limit_bytes=62 << 20),
     )(ensemble, courant_east, northward_courant, perturbation, sensor_cell, measured, error_variance, sensor_count)
+    return pl.pallas_call(
+        unpack_kernel,
+        out_shape=jax.ShapeDtypeStruct((MB, LEV, LON, LAT), F32),
+        in_specs=[hbm],
+        out_specs=hbm,
+        scratch_shapes=[vm(NQ, NB, LON, MB, LAT), vm(MB, LEV, LON, LAT), dma((NQ,)), dma((NQ,))],
+        compiler_params=pltpu.CompilerParams(vmem_limit_bytes=62 << 20),
+    )(back.reshape(2, NB, 2, LON, MB, LAT))
 
 
 def solution(mesh):

time: 65.1 us -> 60.2 us (0.925)
  Pallas kernels: 62.7 us -> 60.1 us
  local copies, waits for them, and re-layouts: 2.3 us -> 0 us
    pallas_call x1 -> x2, Pallas kernels: 62.7 us -> 60.1 us  [the longest x1 56.9 us: on_device(): pl.pallas_call(kernel, out_shape=jax.ShapeDtypeStruct((NG, LON, MB, LAT),...]
    unnamed x1 -> x0, local copies, waits for them, and re-layouts: 2.3 us -> none
where the time goes in v4:
time: 60.2 us; the launch traced here: 60.1 us
  Pallas kernels  60.1 us (100%)
    pallas_call x1, Pallas kernels, on_device(): pl.pallas_call(kernel, out_shape=jax.ShapeDtypeStruct((NG, LON, MB, LAT),...  56.9 us
    pallas_call x1, Pallas kernels, on_device(): pl.pallas_call(unpack_kernel, out_shape=jax.ShapeDtypeStruct((MB, LEV, LO...  3.16 us

profile of v4, /device:TPU:1, one launch (start us, length us, event | category | flops | bytes accessed | tf_op | source)
XLA Modules:
  0.0 60.1 jit_solution(15058783637162716686)
XLA Ops:
  0.0 56.9 %shard_map.82 = f32[16,8,16,128]{3,2,1,0:T(8,128)} custom-call(f32[16,16,8,128]{3,2,1,0:T(8,128)} %ens_hbm.1, f32[16,8,128]{2,1,0:T(8,128)} %ce_hbm.1, f32[16,8,128]{2,1,0:T(8,128)} %cn_hbm.1, f32[16,4,1024]{2,1,0:T(4,128)} %pert_hbm.1, s32[4,1024]{1,0:T(4,128)} %cell_hbm.1, f32[4,1024]{1,0:T(4,128)} %meas_hbm.1, f32[4,1024]{1,0:T(4,128)} %var_hbm.1, s32[4]{0:T(128)} %count_ref.1), custom_call_target="tpu_custom_call" | custom-call | tf_op jit(solution)/shard_map/pallas_call | solution.py:380
  56.9 3.2 %shard_map.83 = f32[16,16,8,128]{3,2,1,0:T(8,128)} custom-call(f32[2,4,2,8,16,128]{5,4,3,2,1,0:T(8,128)} %bitcast.1), custom_call_target="tpu_custom_call" | custom-call | tf_op jit(solution)/shard_map/pallas_call | solution.py:396

commit v5 on v4

--- a/solution.py
+++ b/solution.py
@@ -24,7 +24,7 @@
 HO = NO // 2
 HX = LON // 2
 SCALE = 1.0 / math.sqrt(M - 1)
-UNROLL = 4
+UNROLL = 2
 NR = NG // 2
 MR = NR * MB
 
@@ -56,6 +56,14 @@
 
 def right3(p):
     return jnp.concatenate([p[0], p[1], p[0]], axis=0)
+
+
+def left5(p):
+    return jnp.concatenate([p[0], p[0], p[0], p[1], p[1]], axis=1)
+
+
+def right5(p):
+    return jnp.concatenate([p[0], p[1], p[2], p[0], p[1]], axis=0)
 
 
 def left6(p):
@@ -104,17 +112,19 @@
     east, west = lax.rem(s + 1, NS), lax.rem(s + NS - 1, NS)
     mine = pl.ds(g * MB, MB)
 
-    barrier = pltpu.get_barrier_semaphore()
-    for i in range(1, NG):
-        pl.semaphore_signal(barrier, inc=1, device_id={"grp": lax.rem(g + i, NG)}, device_id_type=MESH)
-    for n in (east, west):
-        pl.semaphore_signal(barrier, inc=1, device_id={"lon": n}, device_id_type=MESH)
-
     loads = []
     for i, (src, dst) in enumerate(((ens_hbm, ens), (pert_hbm, pert), (ce_hbm, ce), (cn_hbm, cn),
                                     (cell_hbm, cell_ref), (meas_hbm, meas), (var_hbm, var))):
         loads.append(pltpu.make_async_copy(src, dst, load.at[i]))
-        loads[-1].start()
+    loads[0].start()
+
+    barrier = pltpu.get_barrier_semaphore()
+    for n in (east, west):
+        pl.semaphore_signal(barrier, inc=1, device_id={"lon": n}, device_id_type=MESH)
+    for i in range(1, NG):
+        pl.semaphore_signal(barrier, inc=1, device_id={"grp": lax.rem(g + i, NG)}, device_id_type=MESH)
+    for c in loads[1:]:
+        c.start()
 
     def remote(src, dst, send, recv, to):
         return pltpu.make_async_remote_copy(
@@ -291,7 +301,7 @@
         m = [mp[:, i * M:(i + 1) * M] for i in range(3)]
         x = split3(inv[...])
         r = (1.0 + low) * eye - (mul(left6(x), right6(m)) if exact else mul(left3(x), right3(m)))
-        inv[...] = k * mul(left6(split3(r)), right6(x))
+        inv[...] = k * mul(left5(split2(r)), right5(x))
         return k * low
 
     sums_copy(1).wait_recv()
@@ -302,12 +312,12 @@
     low = lax.fori_loop(0, 3, lambda i, low: newton(True, low), low)
     rhs_copy(row).wait_recv()
     rhs_pass(core).start()
-    x = right3(split2(inv[...] * (2.0 / (1.0 + low))))
+    x = right5(split3(inv[...] * (2.0 / (1.0 + low))))
     rhs_pass(1 - core).wait_recv()
     m = right6([mp[:, i * M:(i + 1) * M] for i in range(3)])
-    y = mul(left3(split2(rhs[...])), x)
+    y = mul(left5(split2(rhs[...])), x)
     for _ in range(2):
-        y = y + mul(left3(split2(rhs[...] - mul(left6(split3(y)), m))), x)
+        y = y + mul(left5(split2(rhs[...] - mul(left6(split3(y)), m))), x)
     y0, y1 = split2(y * SCALE)
     lhs = jnp.concatenate([y0, y0, y1], axis=1)
 
@@ -346,31 +356,30 @@
     upper = lane >= 64
     odd = (lane // 32) % 2 == 1
 
-    def load(q):
-        return pltpu.make_async_copy(rb.at[q // 2, :, q % 2], buf.at[q], loaded.at[q])
-
-    def store(q):
-        levels = pl.ds(q * (LEV // NQ), LEV // NQ)
-        return pltpu.make_async_copy(out.at[:, levels], out_hbm.at[:, levels], stored.at[q])
-
-    for q in range(NQ):
-        load(q).start()
+    half = MB // 2
+
+    def load(i):
+        q, rows = i // 2, pl.ds(i % 2 * half, half)
+        return pltpu.make_async_copy(rb.at[q // 2, :, q % 2, :, rows], buf.at[q, :, :, rows], loaded.at[i])
+
+    def store(i):
+        rows, levels = pl.ds(i % 2 * half, half), pl.ds(i // 2 * (LEV // NQ), LEV // NQ)
+        return pltpu.make_async_copy(out.at[rows, levels], out_hbm.at[rows, levels], stored.at[i])
+
+    for i in range(2 * NQ):
+        load(i).start()
     back = buf.reshape(NQ * NB * LON * MB, LAT)
-    for q in range(NQ):
-        load(q).wait()
-
-        @pl.loop(0, MB, step=8)
-        def _(m0):
-            for i in range(8):
-                m = m0 + i
-                tiles = swap_blocks([back[pl.ds((q * NB + b) * LON * MB + m, LON, stride=MB), :] for b in range(NB)],
-                                    upper, odd)
-                for k in range(4):
-                    out[m, 4 * q + k] = tiles[k]
-
-        store(q).start()
-    for q in range(NQ):
-        store(q).wait()
+    for i in range(2 * NQ):
+        q = i // 2
+        load(i).wait()
+        for m in range(i % 2 * half, (i % 2 + 1) * half):
+            tiles = swap_blocks([back[pl.ds((q * NB + b) * LON * MB + m, LON, stride=MB), :] for b in range(NB)],
+                                upper, odd)
+            for k in range(4):
+                out[m, 4 * q + k] = tiles[k]
+        store(i).start()
+    for i in range(2 * NQ):
+        store(i).wait()
 
 
 def on_device(ensemble, courant_east, northward_courant, measured, error_variance, sensor_cell, sensor_count, perturbation):
@@ -398,7 +407,7 @@
         out_shape=jax.ShapeDtypeStruct((MB, LEV, LON, LAT), F32),
         in_specs=[hbm],
         out_specs=hbm,
-        scratch_shapes=[vm(NQ, NB, LON, MB, LAT), vm(MB, LEV, LON, LAT), dma((NQ,)), dma((NQ,))],
+        scratch_shapes=[vm(NQ, NB, LON, MB, LAT), vm(MB, LEV, LON, LAT), dma((2 * NQ,)), dma((2 * NQ,))],
         compiler_params=pltpu.CompilerParams(vmem_limit_bytes=62 << 20),
     )(back.reshape(2, NB, 2, LON, MB, LAT))
 

time: 60.2 us -> 59.9 us (level)
  no operation moved by 1% of the time
where the time goes in v5:
time: 59.9 us; the launch traced here: 59.7 us
  Pallas kernels  59.7 us (100%)
    pallas_call x1, Pallas kernels, on_device(): pl.pallas_call(kernel, out_shape=jax.ShapeDtypeStruct((NG, LON, MB, LAT),...  56.6 us
    pallas_call x1, Pallas kernels, on_device(): pl.pallas_call(unpack_kernel, out_shape=jax.ShapeDtypeStruct((MB, LEV, LO...  3.15 us

profile of v5, /device:TPU:1, one launch (start us, length us, event | category | flops | bytes accessed | tf_op | source)
XLA Modules:
  0.0 59.7 jit_solution(13645297032837842459)
XLA Ops:
  0.0 56.6 %shard_map.82 = f32[16,8,16,128]{3,2,1,0:T(8,128)} custom-call(f32[16,16,8,128]{3,2,1,0:T(8,128)} %ens_hbm.1, f32[16,8,128]{2,1,0:T(8,128)} %ce_hbm.1, f32[16,8,128]{2,1,0:T(8,128)} %cn_hbm.1, f32[16,4,1024]{2,1,0:T(4,128)} %pert_hbm.1, s32[4,1024]{1,0:T(4,128)} %cell_hbm.1, f32[4,1024]{1,0:T(4,128)} %meas_hbm.1, f32[4,1024]{1,0:T(4,128)} %var_hbm.1, s32[4]{0:T(128)} %count_ref.1), custom_call_target="tpu_custom_call" | custom-call | tf_op jit(solution)/shard_map/pallas_call | solution.py:389
  56.6 3.1 %shard_map.83 = f32[16,16,8,128]{3,2,1,0:T(8,128)} custom-call(f32[2,4,2,8,16,128]{5,4,3,2,1,0:T(8,128)} %bitcast.1), custom_call_target="tpu_custom_call" | custom-call | tf_op jit(solution)/shard_map/pallas_call | solution.py:405

commit v6 on v5

--- a/solution.py
+++ b/solution.py
@@ -265,7 +265,6 @@
 
     zr[mine] = zb[my_b, core]
 
-    same_row(lambda src: pert_copy(g, src).wait_recv(), -1)
     others(lambda src: z_copy(g, src).wait_recv(), -1)
     others(lambda to: f_copy(to, g).start(), last=8)
     ft[:, mine, :] = fp[g]
@@ -281,6 +280,7 @@
     zw = z * jnp.where(slot + core * HO < count, 1.0 / var[pl.ds(my_b, 1), o], 0.0)
     own_sums[:M] = dot6(z, zw, ((1,), (1,)))
     sums_copy(0).start()
+    same_row(lambda src: pert_copy(g, src).wait_recv(), -1)
     d = (meas[pl.ds(my_b, 1), o] + pt[...]) - zr[row_rows]
     own_sums[M:] = dot6(d, zw, ((1,), (1,)))
     sums_copy(1).start()

time: 59.9 us -> 59.9 us (level)
  no operation moved by 1% of the time
where the time goes in v6:
time: 59.9 us; the launch traced here: 59.7 us
  Pallas kernels  59.7 us (100%)
    pallas_call x1, Pallas kernels, on_device(): pl.pallas_call(kernel, out_shape=jax.ShapeDtypeStruct((NG, LON, MB, LAT),...  56.6 us
    pallas_call x1, Pallas kernels, on_device(): pl.pallas_call(unpack_kernel, out_shape=jax.ShapeDtypeStruct((MB, LEV, LO...  3.15 us

profile of v6, /device:TPU:1, one launch (start us, length us, event | category | flops | bytes accessed | tf_op | source)
XLA Modules:
  0.0 59.7 jit_solution(4229737182074759831)
XLA Ops:
  0.0 56.6 %shard_map.82 = f32[16,8,16,128]{3,2,1,0:T(8,128)} custom-call(f32[16,16,8,128]{3,2,1,0:T(8,128)} %ens_hbm.1, f32[16,8,128]{2,1,0:T(8,128)} %ce_hbm.1, f32[16,8,128]{2,1,0:T(8,128)} %cn_hbm.1, f32[16,4,1024]{2,1,0:T(4,128)} %pert_hbm.1, s32[4,1024]{1,0:T(4,128)} %cell_hbm.1, f32[4,1024]{1,0:T(4,128)} %meas_hbm.1, f32[4,1024]{1,0:T(4,128)} %var_hbm.1, s32[4]{0:T(128)} %count_ref.1), custom_call_target="tpu_custom_call" | custom-call | tf_op jit(solution)/shard_map/pallas_call | solution.py:389
  56.6 3.1 %shard_map.83 = f32[16,16,8,128]{3,2,1,0:T(8,128)} custom-call(f32[2,4,2,8,16,128]{5,4,3,2,1,0:T(8,128)} %bitcast.1), custom_call_target="tpu_custom_call" | custom-call | tf_op jit(solution)/shard_map/pallas_call | solution.py:405
